TPU v7x, 128 devices: a whole 4x4x4 slice. The times are simulated.
128 devices in a mesh: group: 2 (over core), dev: 64 (over y, z, x).
Axes of the slice: x: 4, y: 4, z: 4, core: 2. Of those that a mesh axis runs over, the one named last changes fastest.
Arguments:
- tokens: bfloat16 [16384, 1024], P(('group', 'dev')), may hold values from -6 to 6
- cotangent: bfloat16 [16384, 1024], P(('group', 'dev')), may hold values from -6 to 6
- expert_ids: int32 [16384, 2], P(('group', 'dev')), may hold values from 0 to 63, as said below
- slot_ids: int32 [16384, 2], P(('group', 'dev')), may hold values from 0 to 7, as said below
- w_qkv: bfloat16 [1024, 3072], replicated, may hold values from -0.1875 to 0.1875
- w_proj: bfloat16 [1024, 1024], replicated, may hold values from -0.1875 to 0.1875
- w_router: bfloat16 [1024, 64], replicated, may hold values from -0.1875 to 0.1875
- w_in: bfloat16 [64, 1024, 4096], P('dev', None, 'group'), may hold values from -0.1875 to 0.1875
- w_out: bfloat16 [64, 4096, 1024], P('dev', 'group'), may hold values from -0.09375 to 0.09375
Outputs:
- layer_out: bfloat16 [16384, 1024], P(('group', 'dev'))
- grad_tokens: bfloat16 [16384, 1024], P(('group', 'dev'))
- grad_qkv: float32 [1024, 3072], P(('group', 'dev'))
- grad_proj: float32 [1024, 1024], P(('group', 'dev'))
- grad_router: float32 [1024, 64], P(('group', 'dev'))
- grad_w_in: bfloat16 [64, 1024, 4096], P('dev', None, 'group')
- grad_w_out: bfloat16 [64, 4096, 1024], P('dev', 'group')
Inputs may be any that keep to these rules, and one draw needn't show every extreme that they name: `expert_ids`: the two experts of a token differ. Among the tokens of one clip, each expert is named at most 8 times, and exactly 8 times by some expert of every clip. `slot_ids`: among the choices of one clip that name the same expert, the slots are distinct and below the number of such choices.
All inputs are finite; a program needn't handle non-finite values.
Results may differ from a plain program's by a relative error of at most 0.025.
Values may be sent and summed in bfloat16 or wider, within the bound.
A program may use at most 192 MiB of HBM per device.

v0:
```python
import jax
import jax.numpy as jnp
from jax import lax
from jax.sharding import PartitionSpec as P

HEADS = 16


def layer_norm(values):
    center = values - jnp.mean(values, axis=-1, keepdims=True)
    spread = jnp.mean(center * center, axis=-1, keepdims=True)
    return center * lax.rsqrt(spread + 1e-05)


def attention_block(clip_rows, w_qkv, w_proj):
    count = clip_rows.shape[0]
    width = clip_rows.shape[1]
    head_size = width // HEADS
    normed = layer_norm(clip_rows.astype(jnp.float32)).astype(jnp.bfloat16)
    qkv = jnp.dot(normed, w_qkv, preferred_element_type=jnp.float32).astype(jnp.bfloat16)
    query = qkv[:, :width].reshape(count, HEADS, head_size)
    keys = qkv[:, width : 2 * width].reshape(count, HEADS, head_size)
    values = qkv[:, 2 * width :].reshape(count, HEADS, head_size)
    scores = jnp.einsum("qhd,khd->hqk", query, keys, preferred_element_type=jnp.float32) / jnp.sqrt(
        jnp.float32(head_size)
    )
    probs = jax.nn.softmax(scores, axis=-1).astype(jnp.bfloat16)
    attended = jnp.einsum("hqk,khd->qhd", probs, values, preferred_element_type=jnp.float32).astype(
        jnp.bfloat16
    )
    attended = attended.reshape(count, width)
    return clip_rows.astype(jnp.float32) + jnp.dot(
        attended, w_proj, preferred_element_type=jnp.float32
    )


def gelu_exact(values):
    return jax.nn.gelu(values, approximate=False)


def expert_trip(send_rows, work):
    experts_n, capacity, width = send_rows.shape
    arrived = lax.all_to_all(send_rows, "dev", split_axis=0, concat_axis=0, tiled=True)
    paired = lax.all_gather(arrived[None], "group", axis=0, tiled=True)
    sum_axis = 0
    flat_rows = paired.reshape(-1, width)
    partial_value, extras = work(flat_rows)
    own_part = lax.psum_scatter(
        partial_value.reshape(paired.shape).astype(jnp.bfloat16),
        "group",
        scatter_dimension=sum_axis,
        tiled=True,
    ).astype(jnp.float32)
    own_part = own_part.reshape(experts_n, capacity, width).astype(jnp.bfloat16)
    returned = lax.all_to_all(own_part, "dev", split_axis=0, concat_axis=0, tiled=True)
    return (returned.reshape(experts_n * capacity, width), extras, flat_rows)


def shards(tokens, cotangent, expert_ids, slot_ids, w_qkv, w_proj, w_router, w_in, w_out):
    experts_n = lax.axis_size("dev")
    tok_rows = tokens.shape[0]
    width = tokens.shape[1]
    capacity = 4 * tok_rows // experts_n
    resid32, attn_pullback = jax.vjp(attention_block, tokens, w_qkv, w_proj)
    resid_f = resid32.astype(jnp.bfloat16).astype(jnp.float32)
    normed, norm_pullback = jax.vjp(layer_norm, resid_f)
    normed_b = normed.astype(jnp.bfloat16)
    logits = jnp.dot(normed_b, w_router, preferred_element_type=jnp.float32)
    choice_hot = (
        expert_ids[:, :, None] == jnp.arange(experts_n, dtype=jnp.int32)[None, None, :]
    ).astype(jnp.float32)
    picked = jnp.sum(logits[:, None, :] * choice_hot, axis=-1)
    mixing = jax.nn.softmax(picked, axis=-1)
    flat_slot = expert_ids * capacity + slot_ids
    slot_range = jnp.arange(experts_n * capacity, dtype=jnp.int32)
    place_first = (slot_range[:, None] == flat_slot[None, :, 0]).astype(jnp.bfloat16)
    place_second = (slot_range[:, None] == flat_slot[None, :, 1]).astype(jnp.bfloat16)
    send_rows = jnp.dot(place_first + place_second, normed_b, preferred_element_type=jnp.float32)
    send_rows = send_rows.astype(jnp.bfloat16).reshape(experts_n, capacity, width)
    w_first = w_in[0]
    w_second = w_out[0]

    def forward_work(rows):
        pre = jnp.dot(rows, w_first, preferred_element_type=jnp.float32)
        hidden = gelu_exact(pre).astype(jnp.bfloat16)
        return (jnp.dot(hidden, w_second, preferred_element_type=jnp.float32), (pre, hidden))

    returned, saved, expert_rows = expert_trip(send_rows, forward_work)
    pre_act, hidden_act = saved
    outputs_pair = jnp.take(returned, flat_slot, axis=0)
    layer_out = (
        resid_f + jnp.sum(mixing[:, :, None] * outputs_pair.astype(jnp.float32), axis=1)
    ).astype(jnp.bfloat16)
    grad = cotangent.astype(jnp.float32)
    d_pair = (mixing[:, :, None] * grad[:, None, :]).astype(jnp.bfloat16)
    d_mix = jnp.sum(grad[:, None, :] * outputs_pair.astype(jnp.float32), axis=-1)
    d_picked = mixing * (d_mix - jnp.sum(mixing * d_mix, axis=-1, keepdims=True))
    d_logits = jnp.sum(d_picked[:, :, None] * choice_hot, axis=1).astype(jnp.bfloat16)
    router_term = jnp.einsum("td,te->de", normed_b, d_logits, preferred_element_type=jnp.float32)
    send_grads = jnp.dot(place_first, d_pair[:, 0], preferred_element_type=jnp.float32)
    send_grads = send_grads + jnp.dot(
        place_second, d_pair[:, 1], preferred_element_type=jnp.float32
    )
    send_grads = send_grads.astype(jnp.bfloat16).reshape(experts_n, capacity, width)

    def backward_work(grad_rows):
        d_hidden = jnp.einsum("rd,fd->rf", grad_rows, w_second, preferred_element_type=jnp.float32)
        _, gelu_pullback = jax.vjp(gelu_exact, pre_act)
        d_pre = gelu_pullback(d_hidden)[0].astype(jnp.bfloat16)
        partial_value = jnp.einsum("rf,df->rd", d_pre, w_first, preferred_element_type=jnp.float32)
        grad_second = jnp.einsum(
            "rf,rd->fd", hidden_act, grad_rows, preferred_element_type=jnp.float32
        )
        grad_first = jnp.einsum("rd,rf->df", expert_rows, d_pre, preferred_element_type=jnp.float32)
        return (partial_value, (grad_first.astype(jnp.bfloat16), grad_second.astype(jnp.bfloat16)))

    returned_grad, expert_grads, _ = expert_trip(send_grads, backward_work)
    d_rows_pair = jnp.take(returned_grad, flat_slot, axis=0).astype(jnp.float32)
    d_normed = jnp.sum(d_rows_pair, axis=1) + jnp.einsum(
        "te,de->td", d_logits, w_router, preferred_element_type=jnp.float32
    )
    d_resid = grad + norm_pullback(d_normed)[0]
    grad_tokens, d_qkv, d_proj = attn_pullback(d_resid)
    terms = (d_qkv.astype(jnp.float32), d_proj.astype(jnp.float32), router_term)
    summed = (
        lax.psum_scatter(terms[0], ("group", "dev"), scatter_dimension=0, tiled=True),
        lax.psum_scatter(terms[1], ("group", "dev"), scatter_dimension=0, tiled=True),
        lax.psum_scatter(terms[2], ("group", "dev"), scatter_dimension=0, tiled=True),
    )
    return (
        layer_out,
        grad_tokens,
        summed[0],
        summed[1],
        summed[2],
        expert_grads[0][None],
        expert_grads[1][None],
    )


def solution(mesh):
    return jax.shard_map(
        shards,
        mesh=mesh,
        in_specs=(
            P(("group", "dev"), None),
            P(("group", "dev"), None),
            P(("group", "dev"), None),
            P(("group", "dev"), None),
            P(),
            P(),
            P(),
            P("dev", None, "group"),
            P("dev", "group", None),
        ),
        out_specs=(
            P(("group", "dev"), None),
            P(("group", "dev"), None),
            P(("group", "dev"), None),
            P(("group", "dev"), None),
            P(("group", "dev"), None),
            P("dev", None, "group"),
            P("dev", "group", None),
        ),
        check_vma=False,
    )
```

profile of v0, /device:TPU:0, one launch (start us, length us, event | category | flops | bytes accessed | tf_op | source)
XLA Modules:
  0.0 1270.3 jit_solution(6196623703417424574)
XLA Ops:
  10.9 4.0 convolution_convert_fusion
  23.1 30.3 %all_to_all.20 = bf16[64,8,1024]{2,1,0:T(8,128)(2,1)} all-to-all(bf16[64,8,1024]{2,1,0:T(8,128)(2,1)S(1)} %fusion.28), channel_id=1, replica_groups=mesh['group'=2,'dev'=64] {'dev'}, dimensions={0} | all-to-all | bytes 2097152 | tf_op jit(solution)/shard_map/all_to_all | solution.py:43
  54.0 8.3 all-gather.5.cloned.1.call-done
  62.4 25.7 %multiply_convert_fusion = (bf16[1024,2048]{1,0:T(8,128)(2,1)S(1)}, f32[1024,2048]{1,0:T(8,128)}, f32[1024,2048]{1,0:T(8,128)}) fusion(bf16[1,1024,2048]{2,1,0:T(8,128)(2,1)} %param.18, bf16[128,8,1024]{2,1,0:T(8,128)(2,1)} %all-gather.5.cloned.1.call-done), kind=kOutput, calls=%fused_computation.6 | convolution fusion | flops 4431282176 | bytes 27262976 | tf_op jit(solution)/shard_map/dot_general | solution.py:84
  88.1 1.9 copy-done.30
  90.0 5.7 fusion.21
  95.7 13.7 %reduce-scatter.5.cloned.1.call-done = bf16[1,64,8,1024]{3,2,1,0:T(8,128)(2,1)} async-done(((bf16[2,64,8,1024]{3,2,1,0:T(8,128)(2,1)}), bf16[1,64,8,1024]{3,2,1,0:T(8,128)(2,1)}) %reduce-scatter.5.cloned.1.call-update) | async-done | bytes 1048592 | tf_op jit(solution)/shard_map/reduce_scatter | solution.py:48
  109.5 10.5 all-to-all-start.1
  130.1 9.3 all-to-all-done.1
  139.4 2.0 gather_fusion
  142.6 2.3 fusion.35
  147.0 22.8 %all_to_all.21 = bf16[64,8,1024]{2,1,0:T(8,128)(2,1)} all-to-all(bf16[64,8,1024]{2,1,0:T(8,128)(2,1)S(1)} %fusion.29), channel_id=1, replica_groups=mesh['group'=2,'dev'=64] {'dev'}, dimensions={0} | all-to-all | bytes 2097152 | tf_op jit(solution)/shard_map/all_to_all | solution.py:43
  170.1 8.7 all-gather.7.cloned.1.call-done
  178.8 12.9 %add_convert_fusion = bf16[1024,2048]{1,0:T(8,128)(2,1)S(1)} fusion(f32[1024,2048]{1,0:T(8,128)} %get-tuple-element.15, f32[1024,2048]{1,0:T(8,128)} %get-tuple-element.27, bf16[1,2048,1024]{2,1,0:T(8,128)(2,1)} %param.19, bf16[128,8,1024]{2,1,0:T(8,128)(2,1)} %all-gather.7.cloned.1.call-done), kind=kOutput, calls=%fused_computation.5 | convolution fusion | flops 4324327424 | bytes 27262976 | tf_op jit(solution)/shard_map/rd,fd->rf/dot_general | solution.py:107
  191.6 2.0 copy-done.31
  193.6 5.7 fusion.24
  199.4 13.8 %reduce-scatter.7.cloned.1.call-done = bf16[1,64,8,1024]{3,2,1,0:T(8,128)(2,1)} async-done(((bf16[2,64,8,1024]{3,2,1,0:T(8,128)(2,1)}), bf16[1,64,8,1024]{3,2,1,0:T(8,128)(2,1)}) %reduce-scatter.7.cloned.1.call-update) | async-done | bytes 1048592 | tf_op jit(solution)/shard_map/reduce_scatter | solution.py:48
  213.1 10.5 all-to-all-start.3
  227.7 2.0 fusion.81
  229.7 13.3 %all-to-all-done.3 = bf16[64,8,1024]{2,1,0:T(8,128)(2,1)S(1)} async-done(((bf16[64,8,1024]{2,1,0:T(8,128)(2,1)}), bf16[64,8,1024]{2,1,0:T(8,128)(2,1)S(1)}, u32[]{:S(2)}, u32[]{:S(2)}) %all-to-all-start.3) | async-done | bytes 1048608 | tf_op jit(solution)/shard_map/all_to_all | solution.py:55
  243.0 2.0 gather_fusion.1
  246.3 2.2 convert_reduce_fusion
  250.6 2.1 fusion.75
  252.8 3.8 convert_convert_fusion.1
  259.1 1.8 copy.69
  267.3 6.5 convert_convert_fusion
  273.9 101.9 %all-reduce.6.cloned.1.call-done = f32[1024,64]{1,0:T(8,128)} async-done(((f32[1024,64]{1,0:T(8,128)}), f32[1024,64]{1,0:T(8,128)}) %all-reduce.6.cloned.1.call-update) | async-done | bytes 262160
  377.0 9.6 convert_bitcast_fusion
  386.6 6.5 convert_bitcast_fusion.1
  393.1 5.1 fusion.47
  399.5 640.6 %reduce-scatter.11.cloned.1.call-done = f32[8,1024]{1,0:T(8,128)} async-done(((f32[1024,1024]{1,0:T(8,128)}), f32[8,1024]{1,0:T(8,128)}) %reduce-scatter.11.cloned.1.call-update) | async-done | bytes 32784 | tf_op jit(solution)/shard_map/reduce_scatter | solution.py:127
  1040.1 223.1 %reduce-scatter.9.cloned.1.call-done = f32[8,3072]{1,0:T(8,128)} async-done(((f32[1024,3072]{1,0:T(8,128)}), f32[8,3072]{1,0:T(8,128)}) %reduce-scatter.9.cloned.1.call-update) | async-done | bytes 98320 | tf_op jit(solution)/shard_map/reduce_scatter | solution.py:126
  (129 shorter events, 45.0 us)
Async XLA Ops:
  7.2 13.2 %copy-start = (bf16[1024,1024]{1,0:T(8,128)(2,1)S(1)}, bf16[1024,1024]{1,0:T(8,128)(2,1)}, u32[]{:S(2)}) copy-start(bf16[1024,1024]{1,0:T(8,128)(2,1)} %param.16) | copy-start | bytes 6291460
  7.2 55.2 %all-gather.5.cloned.1.call-start = ((), (), s32[]{:S(2)}) async-start(), calls=%async_computation.12 | async-start | bytes 3145728 | tf_op jit(solution)/shard_map/all_gather | solution.py:44
  10.8 11.1 copy-start.21
  10.8 11.1 copy-start.22
  10.8 9.6 copy-start.1
  18.9 69.1 %copy-start.5 = (f32[16,128,128]{1,2,0:T(8,128)}, f32[16,128,128]{1,2,0:T(8,128)S(1)}, u32[]{:S(2)}) copy-start(f32[16,128,128]{1,2,0:T(8,128)S(1)} %get-tuple-element.24) | copy-start | bytes 3145732
  19.0 69.1 %copy-start.17 = (f32[16,128]{1,0:T(8,128)}, f32[16,128]{1,0:T(8,128)S(1)}, u32[]{:S(2)}) copy-start(f32[16,128]{1,0:T(8,128)S(1)} %get-tuple-element.23) | copy-start | bytes 24580
  21.0 67.1 %copy-start.20 = (f32[128]{0:T(128)}, f32[128]{0:T(128)S(1)}, u32[]{:S(2)}) copy-start(f32[128]{0:T(128)S(1)} %broadcast_multiply_fusion) | copy-start | bytes 1540
  21.2 66.9 %copy-start.26 = (f32[128]{0:T(128)}, f32[128]{0:T(128)S(1)}, u32[]{:S(2)}) copy-start(f32[128]{0:T(128)S(1)} %multiply_reduce_fusion.1) | copy-start | bytes 1540
  21.8 66.3 %copy-start.23 = (f32[128]{0:T(128)}, f32[128]{0:T(128)S(1)}, u32[]{:S(2)}) copy-start(f32[128]{0:T(128)S(1)} %fusion.65) | copy-start | bytes 1540
  53.4 56.0 %reduce-scatter.5.cloned.1.call-start = ((), (), s32[]{:S(2)}) async-start(), calls=%async_computation.8 | async-start | bytes 3145728 | tf_op jit(solution)/shard_map/reduce_scatter | solution.py:48
  62.4 27.6 %copy-start.27 = (bf16[1,2048,1024]{2,1,0:T(8,128)(2,1)S(1)}, bf16[1,2048,1024]{2,1,0:T(8,128)(2,1)}, u32[]{:S(2)}) copy-start(bf16[1,2048,1024]{2,1,0:T(8,128)(2,1)} %param.19) | copy-start | bytes 12582916
  90.0 35.3 %copy-start.9 = (bf16[1024,64]{0,1:T(8,128)(2,1)S(1)}, bf16[1024,64]{0,1:T(8,128)(2,1)}, u32[]{:S(2)}) copy-start(bf16[1024,64]{0,1:T(8,128)(2,1)} %param.17) | copy-start | bytes 393220
  90.0 36.5 %copy-start.16 = (s32[128,2]{0,1:T(2,128)S(1)}, s32[128,2]{0,1:T(2,128)}, u32[]{:S(2)}) copy-start(s32[128,2]{0,1:T(2,128)} %param.13) | copy-start | bytes 3076
  109.5 29.9 %all-to-all-start.1 = ((bf16[64,8,1024]{2,1,0:T(8,128)(2,1)}), bf16[64,8,1024]{2,1,0:T(8,128)(2,1)S(1)}, u32[]{:S(2)}, u32[]{:S(2)}) async-start(bf16[64,8,1024]{2,1,0:T(8,128)(2,1)} %bitcast.108), calls=%async_computation.2 | async-start | bytes 2097152 | tf_op jit(solution)/shard_map/all_to_all | solution.py:55
  120.0 58.8 %all-gather.7.cloned.1.call-start = ((), (), s32[]{:S(2)}) async-start(), calls=%async_computation.13 | async-start | bytes 3145728 | tf_op jit(solution)/shard_map/all_gather | solution.py:44
  169.8 43.3 %reduce-scatter.7.cloned.1.call-start = ((), (), s32[]{:S(2)}) async-start(), calls=%async_computation.9 | async-start | bytes 3145728 | tf_op jit(solution)/shard_map/reduce_scatter | solution.py:48
  178.8 14.9 %copy-start.28 = (bf16[1,1024,2048]{2,1,0:T(8,128)(2,1)S(1)}, bf16[1,1024,2048]{2,1,0:T(8,128)(2,1)}, u32[]{:S(2)}) copy-start(bf16[1,1024,2048]{2,1,0:T(8,128)(2,1)} %param.18) | copy-start | bytes 12582916
  213.1 29.9 %all-to-all-start.3 = ((bf16[64,8,1024]{2,1,0:T(8,128)(2,1)}), bf16[64,8,1024]{2,1,0:T(8,128)(2,1)S(1)}, u32[]{:S(2)}, u32[]{:S(2)}) async-start(bf16[64,8,1024]{2,1,0:T(8,128)(2,1)} %bitcast.107), calls=%async_computation.5 | async-start | bytes 2097152 | tf_op jit(solution)/shard_map/all_to_all | solution.py:55
  223.6 152.1 %all-reduce.6.cloned.1.call-start = ((), (), s32[]{:S(2)}) async-start(), calls=%async_computation.14 | async-start | bytes 1048576
  229.7 810.4 %reduce-scatter.11.cloned.1.call-start = ((), (), s32[]{:S(2)}) async-start(), calls=%async_computation.11 | async-start | bytes 4227072 | tf_op jit(solution)/shard_map/reduce_scatter | solution.py:127
  245.0 12.5 copy-start.4
  248.5 12.4 copy-start.7
  250.6 12.1 copy-start.18
  256.6 1006.6 %reduce-scatter.9.cloned.1.call-start = ((), (), s32[]{:S(2)}) async-start(), calls=%async_computation.10 | async-start | bytes 12681216 | tf_op jit(solution)/shard_map/reduce_scatter | solution.py:126
  260.9 5.2 copy-start.6
  260.9 5.2 copy-start.14
  377.0 9.6 copy-start.29
  377.0 9.6 copy-start.32
  386.6 6.5 copy-start.11
  386.6 6.5 copy-start.13
  386.6 11.6 copy-start.25
  (10 other events, 10.1 us)
Sparse Core Ops, SparseCore 0:
  53.6 8.7 all-gather.4
  95.9 13.5 reduce-scatter.4
  170.0 8.7 all-gather.6
  199.5 13.6 reduce-scatter.6
  229.8 145.9 all-reduce.5
  378.7 661.3 reduce-scatter.10
  1045.6 217.5 reduce-scatter.8
where the time goes:
time: 1270 us
  waiting for transfers between devices  1030 us (81%)
  matrix products  103 us (8%)
  blocking collectives  53.2 us (4%)
  local copies, waits for them, and re-layouts  23.5 us (2%)
  starting transfers between devices  22.1 us (2%)
  other arithmetic  20.6 us (2%)
  between operations  14.9 us (1%)
    reduce_scatter x1, waiting for transfers between devices, shards(): lax.psum_scatter(terms[1], ('group', 'dev'), scatter_dimension=0, tiled=T...  641 us
    reduce_scatter x1, waiting for transfers between devices, shards(): lax.psum_scatter(terms[0], ('group', 'dev'), scatter_dimension=0, tiled=T...  223 us
    unnamed x8, waiting for transfers between devices  102 us
    all_to_all x2, blocking collectives, expert_trip(): lax.all_to_all(send_rows, 'dev', split_axis=0, concat_axis=0, tiled=True)  53.2 us
    reduce_scatter x2, waiting for transfers between devices, expert_trip(): lax.psum_scatter(partial_value.reshape(paired.shape).astype(jnp.bfloat16)...  27.5 us
    dot_general x1, matrix products, forward_work(): pre = jnp.dot(rows, w_first, preferred_element_type=jnp.float32)  25.7 us
  transfers between devices with their start and end apart: 9, of which 9 were waited for; matrix products, arithmetic and copies ran while one was open for 5% of the time, Pallas kernels for 0%

commit v1 on v0

v1 whole, which is shorter than its diff:
```python
import jax
import jax.numpy as jnp
from jax import lax
from jax.experimental import pallas as pl
from jax.experimental.pallas import tpu as pltpu
from jax.sharding import PartitionSpec as P

HEADS = 16
MESH = pl.DeviceIdType.MESH
BF16 = jnp.bfloat16
F32 = jnp.float32
SWAP = [(0, 1), (1, 0)]
VMEM = pl.BlockSpec(memory_space=pltpu.VMEM)
ANY = pl.BlockSpec(memory_space=pl.ANY)
CHUNK = 512


def peer_of(me, k):
    y = (me // 16 + k // 16) % 4
    z = (me // 4 + k // 4) % 4
    x = (me + k) % 4
    return y * 16 + z * 4 + x


def dot(a, b):
    return jnp.dot(a, b, preferred_element_type=F32)


def dot_t(a, b):
    return lax.dot_general(a, b, (((1,), (1,)), ((), ())), preferred_element_type=F32)


def t_dot(a, b):
    return lax.dot_general(a, b, (((0,), (0,)), ((), ())), preferred_element_type=F32)


def expert_kernel(*refs):
    x_in, g_in, m_in, w1_own, w2_own, w1_sib, w2_sib = refs[:7]
    ret_out, ret_in, grad_w1, grad_w2 = refs[7:11]
    w1, w2, xs, gs, xm, gm, hid, dp, acc, pack_out, pack_in = refs[11:22]
    xm_sib, gm_sib, hid_sib, dp_sib, x_turn, stage1, stage2 = refs[22:29]
    w_sem, send_out, recv_out, send_in, recv_in, own_sem, sib_send, sib_recv, grad_sem = refs[29:38]
    g = lax.axis_index("group")
    me = lax.axis_index("dev")
    barrier = pltpu.get_barrier_semaphore()

    def greet(k, _):
        pl.semaphore_signal(barrier, inc=1, device_id=(g, peer_of(me, k)), device_id_type=MESH)
        return 0

    lax.fori_loop(1, 64, greet, 0)
    pl.semaphore_signal(barrier, inc=1, device_id=(1 - g, me), device_id_type=MESH)

    def load(c, own):
        first, second = (w1_own, w2_own) if own else (w1_sib, w2_sib)
        at = pl.ds(pl.multiple_of((c % 4) * CHUNK, CHUNK), CHUNK)
        return (
            pltpu.make_async_copy(first.at[:, at], w1.at[c], w_sem.at[2 * c]),
            pltpu.make_async_copy(second.at[at, :], w2.at[c], w_sem.at[2 * c + 1]),
        )

    for c in range(8):
        for one in load(c, c >= 4):
            one.start()

    lane = lax.broadcasted_iota(jnp.int32, (8, 8, 128), 2)
    slot = lax.broadcasted_iota(jnp.int32, (8, 8, 128), 1)

    def unpack(i, _):
        chips = pl.ds(i * 8, 8)
        rows = pl.ds(pl.multiple_of(i * 64, 64), 64)
        spread = jnp.broadcast_to(m_in[chips], (8, 8, 128))
        mix = jnp.sum(jnp.where(lane == slot, spread, 0.0), axis=2, keepdims=True)
        for src, plain, mixed in ((x_in, xs, xm), (g_in, gs, gm)):
            block = src[chips].astype(F32)
            for h in range(2):
                piece = block[:, h * 8 : h * 8 + 8, :]
                columns = pl.ds(h * 512, 512)
                plain[rows, columns] = piece.reshape(64, 512).astype(BF16)
                mixed[rows, columns] = (piece * mix).reshape(64, 512).astype(BF16)
        return 0

    lax.fori_loop(0, 8, unpack, 0)
    pl.semaphore_wait(barrier, 64)

    def to_sibling(i, src, dst):
        c = pltpu.make_async_remote_copy(
            src_ref=src,
            dst_ref=dst,
            send_sem=sib_send.at[i],
            recv_sem=sib_recv.at[i],
            device_id=(1 - g, me),
            device_id_type=MESH,
        )
        c.start()
        return c

    swaps = [to_sibling(0, xm, xm_sib), to_sibling(1, gm, gm_sib)]

    def forward(c):
        for r in range(2):
            rows = pl.ds(r * 256, 256)
            pre = dot(xs[rows, :], w1[c])
            cdf = 0.5 * (1.0 + lax.erf(pre * (0.5**0.5)))
            pdf = jnp.exp(-0.5 * pre * pre) * 0.3989422804014327
            hid[c, rows, :] = (pre * cdf).astype(BF16)
            dp[c, rows, :] = (cdf + pre * pdf).astype(BF16)
        for r in range(2):
            rows = pl.ds(r * 256, 256)
            acc[rows, :] += dot(hid[c, rows, :], w2[c])

    def backward(c):
        for r in range(2):
            rows = pl.ds(r * 256, 256)
            d_hidden = dot_t(gs[rows, :], w2[c])
            dp[c, rows, :] = (dp[c, rows, :].astype(F32) * d_hidden).astype(BF16)
        for r in range(2):
            rows = pl.ds(r * 256, 256)
            acc[rows, :] += dot_t(dp[c, rows, :], w1[c])

    def pack_into(target):
        def one(i, _):
            value = acc[pl.ds(pl.multiple_of(i * 64, 64), 64), :].reshape(8, 8, 1024)
            both = jnp.concatenate([value[:, :, :512], value[:, :, 512:]], axis=1)
            target[pl.ds(i * 8, 8)] = both.astype(BF16)
            return 0

        lax.fori_loop(0, 8, one, 0)

    def home(k, src, dst, send_sem, recv_sem):
        peer = peer_of(me, k)
        return pltpu.make_async_remote_copy(
            src_ref=src.at[peer],
            dst_ref=dst.at[me],
            send_sem=send_sem.at[k],
            recv_sem=recv_sem.at[k],
            device_id=(g, peer),
            device_id_type=MESH,
        )

    def send_all(src, dst, send_sem, recv_sem, own):
        def one(k, _):
            home(k, src, dst, send_sem, recv_sem).start()
            return 0

        lax.fori_loop(1, 64, one, 0)
        mine = pltpu.make_async_copy(src.at[me], dst.at[me], own_sem.at[own])
        mine.start()
        return mine

    acc[...] = jnp.zeros_like(acc)
    def forward_loop(own):
        def one(c, _):
            for copy in load(c, own):
                copy.wait()
            forward(c)
            return 0

        lax.fori_loop(4 * own, 4 * own + 4, one, 0)

    def backward_loop(own):
        def one(c, _):
            backward(c)
            return 0

        lax.fori_loop(4 * own, 4 * own + 4, one, 0)

    forward_loop(0)
    swaps.append(to_sibling(2, hid.at[pl.ds(0, 4)], hid_sib))
    forward_loop(1)
    pack_into(pack_out)
    mine_out = send_all(pack_out, ret_out, send_out, recv_out, 0)
    acc[...] = jnp.zeros_like(acc)
    backward_loop(0)
    swaps.append(to_sibling(3, dp.at[pl.ds(0, 4)], dp_sib))
    backward_loop(1)
    pack_into(pack_in)
    mine_in = send_all(pack_in, ret_in, send_in, recv_in, 1)

    for s in swaps:
        s.wait_recv()
    for r in range(4):
        rows = pl.ds(r * 128, 128)
        x_turn[:, pl.ds(r * 128, 128)] = xm[rows, :].T
        x_turn[:, pl.ds(512 + r * 128, 128)] = xm_sib[rows, :].T

    def grad_copy(c, which):
        at = pl.ds(pl.multiple_of(c * CHUNK, CHUNK), CHUNK)
        source = stage1 if which == 0 else stage2
        target = grad_w1.at[:, at] if which == 0 else grad_w2.at[at, :]
        return pltpu.make_async_copy(source, target, grad_sem.at[which])

    def grads(c, _):
        @pl.when(c > 0)
        def _():
            grad_copy(c - 1, 0).wait()

        for r in range(4):
            rows = pl.ds(r * 256, 256)
            stage1[rows, :] = (
                dot(x_turn[rows, pl.ds(0, 512)], dp[4 + c])
                + dot(x_turn[rows, pl.ds(512, 512)], dp_sib[c])
            ).astype(BF16)
        grad_copy(c, 0).start()

        @pl.when(c > 0)
        def _():
            grad_copy(c - 1, 1).wait()

        for r in range(2):
            columns = pl.ds(r * 256, 256)
            stage2[columns, :] = (
                t_dot(hid[4 + c, :, columns], gm[...]) + t_dot(hid_sib[c, :, columns], gm_sib[...])
            ).astype(BF16)
        grad_copy(c, 1).start()
        return 0

    lax.fori_loop(0, 4, grads, 0)
    grad_copy(3, 0).wait()
    grad_copy(3, 1).wait()

    def finish(k, _):
        home(k, pack_out, ret_out, send_out, recv_out).wait()
        home(k, pack_in, ret_in, send_in, recv_in).wait()
        return 0

    lax.fori_loop(1, 64, finish, 0)
    mine_out.wait()
    mine_in.wait()
    for s in swaps:
        s.wait_send()


def run_experts(x_blocks, g_blocks, m_blocks, w1_own, w2_own, w1_sib, w2_sib):
    sem = pltpu.SemaphoreType.DMA
    return pl.pallas_call(
        expert_kernel,
        out_shape=[
            jax.ShapeDtypeStruct((64, 16, 512), BF16),
            jax.ShapeDtypeStruct((64, 16, 512), BF16),
            jax.ShapeDtypeStruct((1024, 2048), BF16),
            jax.ShapeDtypeStruct((2048, 1024), BF16),
        ],
        in_specs=[VMEM] * 3 + [ANY] * 4,
        out_specs=[VMEM] * 2 + [ANY] * 2,
        scratch_shapes=[
            pltpu.VMEM((8, 1024, CHUNK), BF16),
            pltpu.VMEM((8, CHUNK, 1024), BF16),
            pltpu.VMEM((512, 1024), BF16),
            pltpu.VMEM((512, 1024), BF16),
            pltpu.VMEM((512, 1024), BF16),
            pltpu.VMEM((512, 1024), BF16),
            pltpu.VMEM((8, 512, CHUNK), BF16),
            pltpu.VMEM((8, 512, CHUNK), BF16),
            pltpu.VMEM((512, 1024), F32),
            pltpu.VMEM((64, 16, 512), BF16),
            pltpu.VMEM((64, 16, 512), BF16),
            pltpu.VMEM((512, 1024), BF16),
            pltpu.VMEM((512, 1024), BF16),
            pltpu.VMEM((4, 512, CHUNK), BF16),
            pltpu.VMEM((4, 512, CHUNK), BF16),
            pltpu.VMEM((1024, 1024), BF16),
            pltpu.VMEM((1024, CHUNK), BF16),
            pltpu.VMEM((CHUNK, 1024), BF16),
            sem((16,)),
            sem((64,)),
            sem((64,)),
            sem((64,)),
            sem((64,)),
            sem((2,)),
            sem((4,)),
            sem((4,)),
            sem((2,)),
        ],
        compiler_params=pltpu.CompilerParams(
            collective_id=2, has_side_effects=True, vmem_limit_bytes=58 * 2**20
        ),
        name="experts",
    )(x_blocks, g_blocks, m_blocks, w1_own, w2_own, w1_sib, w2_sib)


def norm_parts(rows32):
    center = rows32 - jnp.mean(rows32, axis=-1, keepdims=True)
    rstd = lax.rsqrt(jnp.mean(center * center, axis=-1, keepdims=True) + 1e-05)
    return center * rstd, rstd


def norm_backward(normed, rstd, d_normed):
    mean = jnp.mean(d_normed, axis=-1, keepdims=True)
    along_it = jnp.mean(d_normed * normed, axis=-1, keepdims=True)
    return rstd * (d_normed - mean - normed * along_it)


def head_masks():
    low = lax.broadcasted_iota(jnp.int32, (128, 128), 1) < 64
    return low.astype(F32), 1.0 - low.astype(F32)


def two_heads(pair, masks):
    wide = pair.astype(F32)
    return jnp.concatenate([wide * masks[0], wide * masks[1]], axis=0).astype(BF16)


def softmax_pair(scores):
    out = []
    for h in range(2):
        one = scores[:, h * 128 : h * 128 + 128]
        e = jnp.exp(one - jnp.max(one, axis=-1, keepdims=True))
        out.append(e / jnp.sum(e, axis=-1, keepdims=True))
    return out


def attend_kernel(*refs):
    tokens, cot, ids, slots, ids_row, flat_row, w_qkv_in, w_proj_in, w_router = refs[:9]
    x_got, g_got, m_got, resid_out, qkv, att, mix_out = refs[9:16]
    w_qkv, w_proj, n2b, x_pack, g_pack, m_pack = refs[16:22]
    w_sem, send_sem, recv_sem, own_sem = refs[22:26]
    g = lax.axis_index("group")
    me = lax.axis_index("dev")
    barrier = pltpu.get_barrier_semaphore()

    def greet(k, _):
        pl.semaphore_signal(barrier, inc=1, device_id=(g, peer_of(me, k)), device_id_type=MESH)
        return 0

    lax.fori_loop(1, 64, greet, 0)
    loads = []
    for c in range(6):
        at = pl.ds(c * 512, 512)
        loads.append(pltpu.make_async_copy(w_qkv_in.at[:, at], w_qkv.at[:, at], w_sem.at[c]))
    loads.append(pltpu.make_async_copy(w_proj_in, w_proj, w_sem.at[6]))
    for c in loads:
        c.start()

    def dispatch(src, pack):
        for i in range(4):
            at = lax.broadcasted_iota(jnp.int32, (128, 128), 0) + i * 128
            hit = (at == flat_row[0:1, :]) | (at == flat_row[1:2, :])
            place = hit.astype(F32).astype(BF16)
            halves = [dot(place, src[:, h * 512 : h * 512 + 512]).reshape(16, 8, 512) for h in range(2)]
            pack[pl.ds(i * 16, 16)] = jnp.concatenate(halves, axis=1).astype(BF16)

    packs, gots = (x_pack, g_pack, m_pack), (x_got, g_got, m_got)

    def copy(i, k):
        peer = peer_of(me, k)
        return pltpu.make_async_remote_copy(
            src_ref=packs[i].at[peer],
            dst_ref=gots[i].at[me],
            send_sem=send_sem.at[i, k],
            recv_sem=recv_sem.at[i, k],
            device_id=(g, peer),
            device_id_type=MESH,
        )

    def send_all(i):
        def one(k, _):
            copy(i, k).start()
            return 0

        lax.fori_loop(1, 64, one, 0)
        own = pltpu.make_async_copy(packs[i].at[me], gots[i].at[me], own_sem.at[i])
        own.start()
        return own

    dispatch(cot, g_pack)
    pl.semaphore_wait(barrier, 63)
    owns = [send_all(1)]

    rows32 = tokens[...].astype(F32)
    normed, _ = norm_parts(rows32)
    normed_b = normed.astype(BF16)
    for c in range(6):
        loads[c].wait()
        at = pl.ds(c * 512, 512)
        qkv[:, at] = dot(normed_b, w_qkv[:, at]).astype(BF16)
    masks = head_masks()
    for p in range(8):
        q2, k2, v2 = (qkv[:, i * 1024 + p * 128 : i * 1024 + p * 128 + 128] for i in range(3))
        probs = softmax_pair(dot_t(q2, two_heads(k2, masks)) * 0.125)
        probs = jnp.concatenate(probs, axis=1).astype(BF16)
        att[:, p * 128 : p * 128 + 128] = dot(probs, two_heads(v2, masks)).astype(BF16)
    loads[6].wait()
    resid = (rows32 + dot(att[...], w_proj[...])).astype(BF16)
    resid_out[...] = resid
    normed2, _ = norm_parts(resid.astype(F32))
    n2b[...] = normed2.astype(BF16)
    dispatch(n2b, x_pack)
    owns.append(send_all(0))

    logits = dot(n2b[...], w_router[...])
    expert = lax.broadcasted_iota(jnp.int32, (128, 64), 1)
    picked = [
        jnp.sum(jnp.where(expert == ids[:, k : k + 1], logits, 0.0), axis=-1, keepdims=True)
        for k in range(2)
    ]
    top = jnp.maximum(picked[0], picked[1])
    e = [jnp.exp(a - top) for a in picked]
    lane = lax.broadcasted_iota(jnp.int32, (128, 128), 1)
    owner = lax.broadcasted_iota(jnp.int32, (64, 128), 0)
    table = jnp.zeros((64, 128), F32)
    for k in range(2):
        mix = e[k] / (e[0] + e[1])
        mix_out[:, k : k + 1] = mix
        spread = jnp.where(lane == slots[:, k : k + 1], mix, 0.0)
        high = spread.astype(BF16)
        low = (spread - high.astype(F32)).astype(BF16)
        hot = (owner == ids_row[k : k + 1, :]).astype(F32).astype(BF16)
        table = table + dot(hot, high) + dot(hot, low)
    m_pack[...] = table.reshape(64, 1, 128)
    owns.append(send_all(2))

    def finish(k, _):
        for i in range(3):
            copy(i, k).wait()
        return 0

    lax.fori_loop(1, 64, finish, 0)
    for c in owns:
        c.wait()


def run_attend(tokens, cot, ids, slots, ids_row, flat_row, w_qkv, w_proj, w_router):
    sem = pltpu.SemaphoreType.DMA
    shape = jax.ShapeDtypeStruct
    return pl.pallas_call(
        attend_kernel,
        out_shape=[
            shape((64, 16, 512), BF16),
            shape((64, 16, 512), BF16),
            shape((64, 1, 128), F32),
            shape((128, 1024), BF16),
            shape((128, 3072), BF16),
            shape((128, 1024), BF16),
            shape((128, 2), F32),
        ],
        in_specs=[VMEM] * 6 + [ANY] * 2 + [VMEM],
        out_specs=[VMEM] * 7,
        scratch_shapes=[
            pltpu.VMEM((1024, 3072), BF16),
            pltpu.VMEM((1024, 1024), BF16),
            pltpu.VMEM((128, 1024), BF16),
            pltpu.VMEM((64, 16, 512), BF16),
            pltpu.VMEM((64, 16, 512), BF16),
            pltpu.VMEM((64, 1, 128), F32),
            sem((7,)),
            sem((3, 64)),
            sem((3, 64)),
            sem((3,)),
        ],
        compiler_params=pltpu.CompilerParams(
            collective_id=1, has_side_effects=True, vmem_limit_bytes=40 * 2**20
        ),
        name="attend",
    )(tokens, cot, ids, slots, ids_row, flat_row, w_qkv, w_proj, w_router)


ORDERS = ((16, 4, 1), (4, 1, 16), (1, 16, 4))
EARLY, LATE = 384, 1024


def along(me, stride, k):
    at = (me // stride) % 4
    return me - at * stride + ((at + k) % 4) * stride


def natural_row(order, j):
    row = j % 8
    for at, stride in zip((128, 32, 8), ORDERS[order]):
        row = row + ((j // at) % 4) * (stride * 8)
    return row


def finish_kernel(*refs):
    ret_out, ret_in, tokens, cot, resid, qkv, att, mix, ids, flat, w_qkv_in, w_proj_in, w_router = refs[:13]
    layer_out, grad_tokens, sum_qkv, sum_proj, sum_router = refs[13:18]
    w_qkv, w_proj, rows, half_in, half_send, lhs, rhs, d_att = refs[18:26]
    parts, first, mid, second, last, third = (refs[26 + 2 * i : 28 + 2 * i] for i in range(6))
    w_sem, pair_send, pair_recv, send_sem, recv_sem = refs[38:43]
    g = lax.axis_index("group")
    me = lax.axis_index("dev")
    barrier = pltpu.get_barrier_semaphore()
    pl.semaphore_signal(barrier, inc=1, device_id=(1 - g, me), device_id_type=MESH)
    for stride in (16, 4, 1):
        for k in (1, 2, 3):
            pl.semaphore_signal(
                barrier, inc=1, device_id=(g, along(me, stride, k)), device_id_type=MESH
            )
    loads = [
        pltpu.make_async_copy(w_proj_in, w_proj, w_sem.at[0]),
        pltpu.make_async_copy(w_qkv_in, w_qkv, w_sem.at[1]),
    ]
    for c in loads:
        c.start()

    started = []

    def swap(i, src, dst):
        c = pltpu.make_async_remote_copy(
            src_ref=src,
            dst_ref=dst,
            send_sem=pair_send.at[i],
            recv_sem=pair_recv.at[i],
            device_id=(1 - g, me),
            device_id_type=MESH,
        )
        c.start()
        started.append(c)
        return c

    normed1, rstd1 = norm_parts(tokens[...].astype(F32))
    resid_f = resid[...].astype(F32)
    normed2, rstd2 = norm_parts(resid_f)
    half_in[0] = normed1.astype(BF16)
    half_in[1] = att[...]
    half_in[2] = normed2.astype(BF16)
    column = lax.broadcasted_iota(jnp.int32, (512, 512), 1)
    position = lax.broadcasted_iota(jnp.int32, (512, 512), 0)
    mine = pl.ds(pl.multiple_of(g * 512, 512), 512)
    theirs = pl.ds(pl.multiple_of((1 - g) * 512, 512), 512)
    for order in range(3):
        turn = (column == natural_row(order, position)).astype(F32).astype(BF16)
        for which in range(3):
            if which == 2 and order < 2:
                continue
            i = order * 2 + which
            lhs[i, :, 0:128] = dot_t(turn, half_in[which, :, mine]).astype(BF16)
            half_send[i] = dot_t(turn, half_in[which, :, theirs]).astype(BF16)
    pl.semaphore_wait(barrier, 10)
    lhs_swap = [swap(i, half_send.at[i], lhs.at[i, :, pl.ds(128, 128)]) for i in range(7)]

    def unpack(src):
        def one(i, _):
            block = src[pl.ds(i * 8, 8)].astype(F32)
            at = pl.ds(pl.multiple_of(i * 64, 64), 64)
            for h in range(2):
                piece = block[:, h * 8 : h * 8 + 8, :].reshape(64, 512)
                rows[at, pl.ds(h * 512, 512)] = piece.astype(BF16)
            return 0

        lax.fori_loop(0, 8, one, 0)

    slot = lax.broadcasted_iota(jnp.int32, (128, 512), 1)
    place = jnp.concatenate(
        [(slot == flat[:, k : k + 1]).astype(F32).astype(BF16) for k in range(2)], axis=0
    )
    grad = cot[...].astype(F32)
    mixing = [mix[:, k : k + 1] for k in range(2)]
    unpack(ret_out)
    pair = dot(place, rows[...])
    pair = [pair[:128], pair[128:]]
    layer_out[...] = (resid_f + mixing[0] * pair[0] + mixing[1] * pair[1]).astype(BF16)
    d_mix = [jnp.sum(grad * a, axis=-1, keepdims=True) for a in pair]
    centre = mixing[0] * d_mix[0] + mixing[1] * d_mix[1]
    expert = lax.broadcasted_iota(jnp.int32, (128, 128), 1)
    d_logits = sum(
        jnp.where(expert == ids[:, k : k + 1], mixing[k] * (d_mix[k] - centre), 0.0) for k in range(2)
    ).astype(BF16)
    unpack(ret_in)
    pair = dot(place, rows[...])
    d_normed2 = (
        mixing[0] * pair[:128] + mixing[1] * pair[128:] + dot_t(d_logits[:, :64], w_router[...])
    )
    d_resid = grad + norm_backward(normed2, rstd2, d_normed2)
    own_rows, sib_rows = pl.ds(0, 128), pl.ds(128, 128)
    rhs[own_rows, pl.ds(3072, 1024)] = d_resid.astype(BF16)
    rhs[own_rows, pl.ds(4096, 128)] = d_logits
    tail = pl.ds(3072, 1152)
    early_swap = swap(7, rhs.at[own_rows, tail], rhs.at[sib_rows, tail])
    loads[0].wait()
    d_att[...] = dot_t(rhs[own_rows, pl.ds(3072, 1024)], w_proj[...]).astype(BF16)

    def place_of(phase, order):
        return (me // ORDERS[order][phase]) % 4

    def launch(phase, late, order, src, dst):
        stride = ORDERS[order][phase]
        at = place_of(phase, order)
        group = []
        for k in (1, 2, 3):
            sem = ((phase * 2 + late) * 3 + order) * 3 + k - 1
            c = pltpu.make_async_remote_copy(
                src_ref=src.at[order, (at + k) % 4],
                dst_ref=dst.at[order, k - 1],
                send_sem=send_sem.at[sem],
                recv_sem=recv_sem.at[sem],
                device_id=(g, along(me, stride, k)),
                device_id_type=MESH,
            )
            c.start()
            group.append(c)
        started.extend(group)
        return group

    def sum_one(late, order, arriving):
        for c in arriving:
            c.wait_recv()
        at = place_of(0, order)
        for q in range(4):
            piece = pl.ds(q * 32, 32)
            total = parts[late][order, at, piece, :].astype(F32)
            for k in range(3):
                total = total + first[late][order, k, piece, :].astype(F32)
            mid[late][order, q] = total.astype(BF16)
        return launch(1, late, order, mid[late], second[late])

    def sum_two(late, order, arriving):
        for c in arriving:
            c.wait_recv()
        total = mid[late][order, place_of(1, order)].astype(F32)
        for k in range(3):
            total = total + second[late][order, k].astype(F32)
        for q in range(4):
            last[late][order, q] = total[q * 8 : q * 8 + 8, :]
        return launch(2, late, order, last[late], third[late])

    def sum_three(late, order, arriving):
        for c in arriving:
            c.wait_recv()
        total = last[late][order, place_of(2, order)]
        for k in range(3):
            total = total + third[late][order, k]
        return total

    for c in lhs_swap:
        c.wait_recv()
    early_swap.wait_recv()
    early = []
    for order in range(3):
        for r in range(4):
            for left, at, width in (
                (order * 2 + 1, 0, EARLY if order < 2 else 256),
                (6, 256, 128),
            ):
                if left == 6 and order < 2:
                    continue
                value = dot(
                    lhs[left, r * 128 : r * 128 + 128, :],
                    rhs[:, 3072 + order * EARLY + at : 3072 + order * EARLY + at + width],
                )
                parts[0][order, r, :, pl.ds(at, width)] = value.astype(BF16)
        early.append(launch(0, 0, order, parts[0], first[0]))

    masks = head_masks()
    for p in range(8):
        q2, k2, v2 = (qkv[:, i * 1024 + p * 128 : i * 1024 + p * 128 + 128] for i in range(3))
        d2 = d_att[:, p * 128 : p * 128 + 128]
        k_two, v_two = two_heads(k2, masks), two_heads(v2, masks)
        probs = softmax_pair(dot_t(q2, k_two) * 0.125)
        d_probs = dot_t(d2, v_two)
        d_scores = []
        for h in range(2):
            one = d_probs[:, h * 128 : h * 128 + 128]
            one = probs[h] * (one - jnp.sum(probs[h] * one, axis=-1, keepdims=True))
            d_scores.append(one * 0.125)
        d_scores = jnp.concatenate(d_scores, axis=1).astype(BF16)
        probs = jnp.concatenate(probs, axis=1).astype(BF16)
        d_k = t_dot(d_scores, q2)
        d_v = t_dot(probs, d2)
        rhs[own_rows, pl.ds(p * 128, 128)] = dot(d_scores, k_two).astype(BF16)
        rhs[own_rows, pl.ds(1024 + p * 128, 128)] = (
            d_k[:128] * masks[0] + d_k[128:] * masks[1]
        ).astype(BF16)
        rhs[own_rows, pl.ds(2048 + p * 128, 128)] = (
            d_v[:128] * masks[0] + d_v[128:] * masks[1]
        ).astype(BF16)
    late_swap = []
    for order in range(3):
        at = pl.ds(order * LATE, LATE)
        late_swap.append(swap(8 + order, rhs.at[own_rows, at], rhs.at[sib_rows, at]))
    early = [sum_one(0, order, early[order]) for order in range(3)]
    late = []
    for order in range(3):
        late_swap[order].wait_recv()
        for r in range(4):
            value = dot(
                lhs[order * 2, r * 128 : r * 128 + 128, :], rhs[:, order * LATE : order * LATE + LATE]
            )
            parts[1][order, r] = value.astype(BF16)
        late.append(launch(0, 1, order, parts[1], first[1]))
    early = [sum_two(0, order, early[order]) for order in range(3)]
    loads[1].wait()
    d_normed1 = dot_t(rhs[own_rows, pl.ds(0, 3072)], w_qkv[...])
    grad_tokens[...] = (d_resid + norm_backward(normed1, rstd1, d_normed1)).astype(BF16)
    late = [sum_one(1, order, late[order]) for order in range(3)]
    sum_proj[:, 0:384] = sum_three(0, 0, early[0])
    sum_proj[:, 384:768] = sum_three(0, 1, early[1])
    tail_sum = sum_three(0, 2, early[2])
    sum_proj[:, 768:1024] = tail_sum[:, :256]
    sum_router[...] = tail_sum[:, 256:320]
    late = [sum_two(1, order, late[order]) for order in range(3)]
    for order in range(3):
        sum_qkv[:, order * LATE : order * LATE + LATE] = sum_three(1, order, late[order])
    for c in started:
        c.wait_send()


def run_finish(*args):
    sem = pltpu.SemaphoreType.DMA
    shape = jax.ShapeDtypeStruct
    scratch = [
        pltpu.VMEM((1024, 3072), BF16),
        pltpu.VMEM((1024, 1024), BF16),
        pltpu.VMEM((512, 1024), BF16),
        pltpu.VMEM((3, 128, 1024), BF16),
        pltpu.VMEM((7, 512, 128), BF16),
        pltpu.VMEM((7, 512, 256), BF16),
        pltpu.VMEM((256, 4224), BF16),
        pltpu.VMEM((128, 1024), BF16),
    ]
    for lead, kind in (
        ((3, 4, 128), BF16),
        ((3, 3, 128), BF16),
        ((3, 4, 32), BF16),
        ((3, 3, 32), BF16),
        ((3, 4, 8), F32),
        ((3, 3, 8), F32),
    ):
        scratch += [pltpu.VMEM(lead + (width,), kind) for width in (EARLY, LATE)]
    scratch += [sem((2,)), sem((11,)), sem((11,)), sem((54,)), sem((54,))]
    return pl.pallas_call(
        finish_kernel,
        out_shape=[
            shape((128, 1024), BF16),
            shape((128, 1024), BF16),
            shape((8, 3072), F32),
            shape((8, 1024), F32),
            shape((8, 64), F32),
        ],
        in_specs=[VMEM] * 10 + [ANY] * 2 + [VMEM],
        out_specs=[VMEM] * 5,
        scratch_shapes=scratch,
        compiler_params=pltpu.CompilerParams(
            collective_id=3, has_side_effects=True, vmem_limit_bytes=48 * 2**20
        ),
        name="finish",
    )(*args)


def shards(tokens, cotangent, expert_ids, slot_ids, w_qkv, w_proj, w_router, w_in, w_out):
    other_in = lax.ppermute(w_in[0], "group", SWAP)
    other_out = lax.ppermute(w_out[0], "group", SWAP)
    flat = expert_ids * 8 + slot_ids
    x_blocks, g_blocks, m_blocks, resid, qkv, att, mix = run_attend(
        tokens, cotangent, expert_ids, slot_ids, expert_ids.T, flat.T, w_qkv, w_proj, w_router
    )
    returned_out, returned_in, grad_w_in, grad_w_out = run_experts(
        x_blocks, g_blocks, m_blocks, w_in[0], w_out[0], other_in, other_out
    )
    layer_out, grad_tokens, sum_qkv, sum_proj, sum_router = run_finish(
        returned_out, returned_in, tokens, cotangent, resid, qkv, att, mix, expert_ids, flat, w_qkv, w_proj, w_router
    )
    return (
        layer_out,
        grad_tokens,
        sum_qkv,
        sum_proj,
        sum_router,
        grad_w_in[None],
        grad_w_out[None],
    )


def solution(mesh):
    return jax.shard_map(
        shards,
        mesh=mesh,
        in_specs=(
            P(("group", "dev"), None),
            P(("group", "dev"), None),
            P(("group", "dev"), None),
            P(("group", "dev"), None),
            P(),
            P(),
            P(),
            P("dev", None, "group"),
            P("dev", "group", None),
        ),
        out_specs=(
            P(("group", "dev"), None),
            P(("group", "dev"), None),
            P(("group", "dev"), None),
            P(("group", "dev"), None),
            P(("group", "dev"), None),
            P("dev", None, "group"),
            P("dev", "group", None),
        ),
        check_vma=False,
    )
```

time: 1270 us -> 162 us (0.13)
  waiting for transfers between devices: 1030 us -> 0.01 us
  Pallas kernels: 0 us -> 136 us
  matrix products: 103 us -> 0 us
  blocking collectives: 53.2 us -> 0 us
  starting transfers between devices: 22.1 us -> 0.58 us
  other arithmetic: 20.6 us -> 0.7 us
  between operations: 14.9 us -> 0.74 us
    reduce_scatter x4 -> x0, waiting for transfers between devices: 891 us -> none  [the longest x1 641 us: shards(): lax.psum_scatter(terms[1], ('group', 'dev'), scatter_dimension=0, tiled=T...]
    pallas_call x0 -> x3, Pallas kernels: none -> 136 us  [the longest x1 52.8 us: run_experts(): pl.pallas_call(expert_kernel, out_shape=[jax.ShapeDtypeStruct((64, 16, 51...]
    unnamed x8 -> x0, waiting for transfers between devices: 102 us -> none
    dot_general x23 -> x0, matrix products: 102 us -> none  [the longest x1 25.7 us: forward_work(): pre = jnp.dot(rows, w_first, preferred_element_type=jnp.float32)]
    all_to_all x2 -> x0, blocking collectives: 53.2 us -> none  [expert_trip(): lax.all_to_all(send_rows, 'dev', split_axis=0, concat_axis=0, tiled=True)]
    all_to_all x2 -> x0, waiting for transfers between devices: 22.6 us -> none  [expert_trip(): lax.all_to_all(own_part, 'dev', split_axis=0, concat_axis=0, tiled=True)]
    all_to_all x2 -> x0, starting transfers between devices: 20.9 us -> none  [expert_trip(): lax.all_to_all(own_part, 'dev', split_axis=0, concat_axis=0, tiled=True)]
    all_gather x2 -> x0, waiting for transfers between devices: 17 us -> none  [expert_trip(): paired = lax.all_gather(arrived[None], 'group', axis=0, tiled=True)]
  transfers between devices with their start and end apart: 9 -> 2, of which waited for: 9 -> 0; matrix products, arithmetic and copies ran while one was open for 5% -> 2% of each run, Pallas kernels for 0% -> 26%
where the time goes in v1:
time: 162 us; the launch traced here: 161 us
  Pallas kernels  136 us (84%)
  local copies, waits for them, and re-layouts  23.7 us (15%)
    pallas_call x1, Pallas kernels, run_experts(): pl.pallas_call(expert_kernel, out_shape=[jax.ShapeDtypeStruct((64, 16, 51...  52.8 us
    pallas_call x1, Pallas kernels, run_attend(): pl.pallas_call(attend_kernel, out_shape=[shape((64, 16, 512), BF16), shap...  42.6 us
    pallas_call x1, Pallas kernels, run_finish(): pl.pallas_call(finish_kernel, out_shape=[shape((128, 1024), BF16), shape(...  40.3 us
    unnamed x38, local copies, waits for them, and re-layouts  23.6 us
  transfers between devices with their start and end apart: 2, of which 0 were waited for; matrix products, arithmetic and copies ran while one was open for 2% of the time, Pallas kernels for 26%

profile of v1, /device:TPU:0, one launch (start us, length us, event | category | flops | bytes accessed | tf_op | source)
XLA Modules:
  0.0 161.4 jit_solution(15636497766292701074)
XLA Ops:
  0.6 0.1 collective-permute-start
  0.7 0.5 collective-permute-start.1
  1.2 1.1 copy.27.refs_8_.refs_12_
  2.3 0.8 copy.25.refs_2_.refs_8_
  3.1 0.8 copy.26.refs_3_
  3.9 0.7 multiply_add_fusion
  4.6 0.1 copy.29.refs_9_
  4.7 2.8 %copy-done = bf16[1024,3072]{1,0:T(8,128)(2,1)S(1)} copy-done((bf16[1024,3072]{1,0:T(8,128)(2,1)S(1)}, bf16[1024,3072]{1,0:T(8,128)(2,1)}, u32[]{:S(2)}) %copy-start) | copy-done | bytes 6291480
  7.5 1.6 copy-done.1
  9.1 0.9 copy-done.6
  10.0 0.9 copy-done.8
  11.0 0.7 copy-done.11
  11.6 42.6 %attend.1 = (bf16[64,16,512]{2,1,0:T(8,128)(2,1)S(1)}, bf16[64,16,512]{2,1,0:T(8,128)(2,1)S(1)}, f32[64,1,128]{2,1,0:T(1,128)S(1)}, bf16[128,1024]{1,0:T(8,128)(...) custom-call(bf16[128,1024]{1,0:T(8,128)(2,1)S(1)} %copy-done.6, ...), custom_call_target="tpu_custom_call" | custom-call | tf_op jit(solution)/shard_map/attend/pallas_call | solution.py:426
  54.2 0.0 copy-start.4
  54.3 1.0 copy-done.4
  55.2 1.0 copy-done.5
  56.2 0.6 copy-done.10
  56.8 0.0 collective-permute-done.refs_5_
  56.8 0.0 collective-permute-done.1.refs_6_
  56.8 0.0 copy-start.9
  56.8 52.8 %experts.1 = (bf16[64,16,512]{2,1,0:T(8,128)(2,1)}, bf16[64,16,512]{2,1,0:T(8,128)(2,1)}, bf16[1024,2048]{1,0:T(8,128)(2,1)}, bf16[2048,1024]{1,0:T(8,128)(2,1)}) custom-call(bf16[64,16,512]{2,1,0:T(8,128)(2,1)} %copy-done.4, bf16[64,16,512]{2,1,0:T(8,128)(2,1)} %copy-done.5, f32[64,1,128]{2,1,0:T(1,128)} %copy-done.10, bf16[1024,2048]{1,0:T(8,128)(2,1)} %bitcast.11, ...), custom_call_target="tpu_custom_call" | custom-call | tf_op jit(solution)/shard_map/experts/pallas_call | solution.py:236
  109.7 1.2 copy-done.2
  110.9 1.2 copy-done.3
  112.1 40.3 %finish.1 = (bf16[128,1024]{1,0:T(8,128)(2,1)S(1)}, bf16[128,1024]{1,0:T(8,128)(2,1)S(1)}, f32[8,3072]{1,0:T(8,128)S(1)}, f32[8,1024]{1,0:T(8,128)S(1)}, f32[8,64]{1,0:T(8,128)S(1)}) custom-call(bf16[64,16,512]{2,1,0:T(8,128)(2,1)S(1)} %copy-done.2, bf16[64,16,512]{2,1,0:T(8,128)(2,1)S(1)} %copy-done.3, bf16[128,1024]{1,0:T(8,128)(2,1)S(1)} %copy-done.7, ...), custom_call_target="tpu_custom_call" | custom-call | tf_op jit(solution)/shard_map/finish/pallas_call | solution.py:721
  152.4 0.7 copy.38
  153.1 0.7 copy.39
  153.8 0.6 copy.40
  154.5 0.6 copy.41
  155.1 0.6 copy.42
  155.7 2.1 %copy.43 = bf16[1,1024,2048]{2,1,0:T(8,128)(2,1)} copy(bf16[1,1024,2048]{2,1,0:T(8,128)(2,1)S(1)} %bitcast.9) | data formatting | bytes 8388608
  157.8 1.6 copy-done.12
  159.4 2.0 %copy.44 = bf16[1,2048,1024]{2,1,0:T(8,128)(2,1)} copy(bf16[1,2048,1024]{2,1,0:T(8,128)(2,1)S(1)} %bitcast.8) | data formatting | bytes 8388608
  (15 shorter events, 0.0 us)
Async XLA Ops:
  0.6 56.2 %collective-permute-start = (bf16[1024,2048]{1,0:T(8,128)(2,1)}, bf16[1024,2048]{1,0:T(8,128)(2,1)}, u32[]{:S(2)}, u32[]{:S(2)}) collective-permute-start(bf16[1024,2048]{1,0:T(8,128)(2,1)} %bitcast.10), channel_id=1, source_target_pairs={{0,64},{64,0},{1,65},{65,1},{2,66},{66,2},{3,67},{67,3},{4,68},{68... | collective-permute-start | bytes 12582920 | tf_op jit(solution)/shard_map/ppermute | solution.py:741
  0.7 56.1 %collective-permute-start.1 = (bf16[2048,1024]{1,0:T(8,128)(2,1)}, bf16[2048,1024]{1,0:T(8,128)(2,1)}, u32[]{:S(2)}, u32[]{:S(2)}) collective-permute-start(bf16[2048,1024]{1,0:T(8,128)(2,1)} %bitcast.12), channel_id=1, source_target_pairs={{0,64},{64,0},{1,65},{65,1},{2,66},{66,2},{3,67},{67,3},{4,68},{68... | collective-permute-start | bytes 12582920 | tf_op jit(solution)/shard_map/ppermute | solution.py:742
  4.7 2.8 %copy-start = (bf16[1024,3072]{1,0:T(8,128)(2,1)S(1)}, bf16[1024,3072]{1,0:T(8,128)(2,1)}, u32[]{:S(2)}) copy-start(bf16[1024,3072]{1,0:T(8,128)(2,1)} %refs_10_.1) | copy-start | bytes 18874372
  7.5 1.6 copy-start.1
  9.1 0.9 copy-start.6
  10.0 0.9 copy-start.8
  11.0 0.7 copy-start.11
  54.2 1.0 copy-start.4
  55.2 1.0 copy-start.5
  56.2 0.6 copy-start.10
  56.8 52.8 %copy-start.7 = (bf16[128,1024]{1,0:T(8,128)(2,1)S(1)}, bf16[128,1024]{1,0:T(8,128)(2,1)}, u32[]{:S(2)}) copy-start(bf16[128,1024]{1,0:T(8,128)(2,1)} %refs_2_.2) | copy-start | bytes 786436
  56.8 52.8 %copy-start.9 = (bf16[128,1024]{1,0:T(8,128)(2,1)S(1)}, bf16[128,1024]{1,0:T(8,128)(2,1)}, u32[]{:S(2)}) copy-start(bf16[128,1024]{1,0:T(8,128)(2,1)} %refs_3_.2) | copy-start | bytes 786436
  109.7 1.2 copy-start.2
  110.9 1.2 copy-start.3
  112.1 43.6 %copy-start.13 = (bf16[1024,2048]{1,0:T(8,128)(2,1)S(1)}, bf16[1024,2048]{1,0:T(8,128)(2,1)}, u32[]{:S(2)}) copy-start(bf16[1024,2048]{1,0:T(8,128)(2,1)} %get-tuple-element.37) | copy-start | bytes 12582916
  155.7 3.7 %copy-start.12 = (bf16[2048,1024]{1,0:T(8,128)(2,1)S(1)}, bf16[2048,1024]{1,0:T(8,128)(2,1)}, u32[]{:S(2)}) copy-start(bf16[2048,1024]{1,0:T(8,128)(2,1)} %get-tuple-element.38) | copy-start | bytes 12582916

commit v2 on v1

v2 whole, which is shorter than its diff:
```python
import jax
import jax.numpy as jnp
from jax import lax
from jax.experimental import pallas as pl
from jax.experimental.pallas import tpu as pltpu
from jax.sharding import PartitionSpec as P

HEADS = 16
MESH = pl.DeviceIdType.MESH
BF16 = jnp.bfloat16
F32 = jnp.float32
VMEM = pl.BlockSpec(memory_space=pltpu.VMEM)
HBM = pl.BlockSpec(memory_space=pltpu.HBM)
CHUNK = 512


def peer_of(me, k):
    y = (me // 16 + k // 16) % 4
    z = (me // 4 + k // 4) % 4
    x = (me + k) % 4
    return y * 16 + z * 4 + x


def offset_of(j):
    r = j % 32
    y = r // 8
    z = (r // 2) % 4
    x = 2 * (r % 2) + (y + z + j // 32) % 2
    return y * 16 + z * 4 + x


def chip_before(me, k):
    y = (me // 16 + 4 - k // 16) % 4
    z = (me // 4 + 4 - (k // 4) % 4) % 4
    x = (me + 4 - k % 4) % 4
    return y * 16 + z * 4 + x


def dot(a, b):
    return jnp.dot(a, b, preferred_element_type=F32)


def dot_t(a, b):
    return lax.dot_general(a, b, (((1,), (1,)), ((), ())), preferred_element_type=F32)


def t_dot(a, b):
    return lax.dot_general(a, b, (((0,), (0,)), ((), ())), preferred_element_type=F32)


def norm_parts(rows32):
    center = rows32 - jnp.mean(rows32, axis=-1, keepdims=True)
    rstd = lax.rsqrt(jnp.mean(center * center, axis=-1, keepdims=True) + 1e-05)
    return center * rstd, rstd


def norm_backward(normed, rstd, d_normed):
    mean = jnp.mean(d_normed, axis=-1, keepdims=True)
    along_it = jnp.mean(d_normed * normed, axis=-1, keepdims=True)
    return rstd * (d_normed - mean - normed * along_it)


def head_masks():
    low = lax.broadcasted_iota(jnp.int32, (128, 128), 1) < 64
    return low.astype(F32), 1.0 - low.astype(F32)


def two_heads(pair, masks):
    wide = pair.astype(F32)
    return jnp.concatenate([wide * masks[0], wide * masks[1]], axis=0).astype(BF16)


def softmax_pair(scores):
    out = []
    for h in range(2):
        one = scores[:, h * 128 : h * 128 + 128]
        e = jnp.exp(one - jnp.max(one, axis=-1, keepdims=True))
        out.append(e / jnp.sum(e, axis=-1, keepdims=True))
    return out


def columns_of(row_ref):
    rows = row_ref[...].astype(F32)
    return [jnp.broadcast_to(rows[k : k + 1, :], (128, 128)).T.astype(jnp.int32) for k in range(2)]


def layer_kernel(*refs):
    tokens_in, cot_in, ids_in, slots_in, w_qkv_in, w_proj_in, w_router_in, w1_own, w2_own = refs[:9]
    ret_out, ret_in, resid_out, qkv_out, att_out, mix_out, grad_w1, grad_w2 = refs[9:17]
    tokens, cot, ids_row, slots_row, w_router, resid_buf, qkv, att, mix_buf = refs[17:26]
    w_qkv, w_proj, n2b, x_pack, g_pack, m_pack = refs[26:32]
    w1, w2, xs, gs, xm, gm, hid, dp, acc, pack_out, pack_in = refs[32:43]
    xm_sib, gm_sib, hid_sib, dp_sib, x_turn, stage1, stage2, x_buf, g_buf, m_buf = refs[43:53]
    in_sem, w_sem, push_send, push_recv, send_sem, recv_sem, home_send, home_recv = refs[53:61]
    own_sem, out_sem, sib_send, sib_recv, grad_sem = refs[61:66]
    g = lax.axis_index("group")
    me = lax.axis_index("dev")
    barrier = pltpu.get_barrier_semaphore()
    pl.semaphore_signal(barrier, inc=1, device_id=(1 - g, me), device_id_type=MESH)

    def greet(k, _):
        pl.semaphore_signal(barrier, inc=1, device_id=(g, peer_of(me, k)), device_id_type=MESH)
        return 0

    lax.fori_loop(1, 64, greet, 0)
    fetch = [
        pltpu.make_async_copy(src, dst, in_sem.at[7 + i])
        for i, (src, dst) in enumerate(
            (
                (ids_in, ids_row),
                (slots_in, slots_row),
                (cot_in, cot),
                (tokens_in, tokens),
                (w_router_in, w_router),
            )
        )
    ]
    loads = []
    for c in range(6):
        at = pl.ds(c * 512, 512)
        loads.append(pltpu.make_async_copy(w_qkv_in.at[:, at], w_qkv.at[:, at], in_sem.at[c]))
    loads.append(pltpu.make_async_copy(w_proj_in, w_proj, in_sem.at[6]))
    for c in fetch[:4] + loads + fetch[4:]:
        c.start()

    started = []

    def to_sibling(src, dst, send, recv):
        c = pltpu.make_async_remote_copy(
            src_ref=src,
            dst_ref=dst,
            send_sem=send,
            recv_sem=recv,
            device_id=(1 - g, me),
            device_id_type=MESH,
        )
        c.start()
        started.append(c)
        return c

    def weights(c):
        at = pl.ds(c * CHUNK, CHUNK)
        return w1_own.at[:, at], w2_own.at[at, :]

    def dispatch(src, pack):
        for i in range(4):
            at = lax.broadcasted_iota(jnp.int32, (128, 128), 0) + i * 128
            hit = (at == flat_row[0:1, :]) | (at == flat_row[1:2, :])
            place = hit.astype(F32).astype(BF16)
            halves = [dot(place, src[:, h * 512 : h * 512 + 512]).reshape(16, 8, 512) for h in range(2)]
            pack[pl.ds(i * 16, 16)] = jnp.concatenate(halves, axis=1).astype(BF16)

    packs, bufs = (x_pack, g_pack, m_pack), (x_buf, g_buf, m_buf)

    def out_copy(i, j):
        peer = peer_of(me, offset_of(j))
        return pltpu.make_async_remote_copy(
            src_ref=packs[i].at[peer],
            dst_ref=bufs[i].at[j],
            send_sem=send_sem.at[i, j],
            recv_sem=recv_sem.at[i, j],
            device_id=(g, peer),
            device_id_type=MESH,
        )

    def own_copy(i):
        return pltpu.make_async_copy(packs[i].at[me], bufs[i].at[0], own_sem.at[i])

    def over(low, high, action):
        def one(j, _):
            action(j)
            return 0

        lax.fori_loop(low, high, one, 0)

    def send_out(i, half):
        if half == 0:
            own_copy(i).start()
        over(1 + 31 * half, 32 + 32 * half, lambda j: out_copy(i, j).start())

    def take_in(i, half):
        if half == 0:
            own_copy(i).wait()
        over(1 + 31 * half, 32 + 32 * half, lambda j: out_copy(i, j).wait_recv())

    for c in fetch[:3]:
        c.wait()
    flat_row = ids_row[...] * 8 + slots_row[...]
    dispatch(cot, g_pack)
    pl.semaphore_wait(barrier, 64)
    send_out(1, 0)
    pushes = []
    for c in range(4):
        for i, (src, dst) in enumerate(zip(weights(c), (w1, w2))):
            sem = 2 * c + i
            pushes.append(to_sibling(src, dst.at[c], push_send.at[sem], push_recv.at[sem]))
    own_loads = []
    for c in range(4):
        for i, (src, dst) in enumerate(zip(weights(c), (w1, w2))):
            own_loads.append(pltpu.make_async_copy(src, dst.at[4 + c], w_sem.at[2 * c + i]))
            own_loads[-1].start()

    fetch[3].wait()
    rows32 = tokens[...].astype(F32)
    normed, _ = norm_parts(rows32)
    normed_b = normed.astype(BF16)
    for c in range(6):
        loads[c].wait()
        at = pl.ds(c * 512, 512)
        qkv[:, at] = dot(normed_b, w_qkv[:, at]).astype(BF16)
    masks = head_masks()
    for p in range(8):
        q2, k2, v2 = (qkv[:, i * 1024 + p * 128 : i * 1024 + p * 128 + 128] for i in range(3))
        probs = softmax_pair(dot_t(q2, two_heads(k2, masks)) * 0.125)
        probs = jnp.concatenate(probs, axis=1).astype(BF16)
        att[:, p * 128 : p * 128 + 128] = dot(probs, two_heads(v2, masks)).astype(BF16)
    loads[6].wait()
    resid = (rows32 + dot(att[...], w_proj[...])).astype(BF16)
    resid_buf[...] = resid
    normed2, _ = norm_parts(resid.astype(F32))
    n2b[...] = normed2.astype(BF16)
    dispatch(n2b, x_pack)
    send_out(0, 0)
    send_out(0, 1)

    leaving = [
        pltpu.make_async_copy(src, dst, out_sem.at[i])
        for i, (src, dst) in enumerate(((resid_buf, resid_out), (qkv, qkv_out), (att, att_out)))
    ]
    for c in leaving:
        c.start()
    fetch[4].wait()
    logits = dot_t(n2b[...], w_router[...])
    ids, slots = columns_of(ids_row), columns_of(slots_row)
    expert = lax.broadcasted_iota(jnp.int32, (128, 64), 1)
    picked = [
        jnp.sum(jnp.where(expert == ids[k][:, :64], logits, 0.0), axis=-1, keepdims=True)
        for k in range(2)
    ]
    top = jnp.maximum(picked[0], picked[1])
    e = [jnp.exp(a - top) for a in picked]
    lane = lax.broadcasted_iota(jnp.int32, (128, 128), 1)
    owner = lax.broadcasted_iota(jnp.int32, (64, 128), 0)
    table = jnp.zeros((64, 128), F32)
    for k in range(2):
        mix = e[k] / (e[0] + e[1])
        mix_buf[:, k * 128 : k * 128 + 128] = jnp.broadcast_to(mix, (128, 128))
        spread = jnp.where(lane == slots[k], mix, 0.0)
        high = spread.astype(BF16)
        low = (spread - high.astype(F32)).astype(BF16)
        hot = (owner == ids_row[k : k + 1, :]).astype(F32).astype(BF16)
        table = table + dot(hot, high) + dot(hot, low)
    m_pack[...] = table.reshape(64, 1, 128)
    send_out(2, 0)
    send_out(2, 1)
    send_out(1, 1)
    leaving.append(pltpu.make_async_copy(mix_buf, mix_out, out_sem.at[3]))
    leaving[3].start()

    def unpack(i, half, plain):
        def one(b):
            block = bufs[i][pl.ds(b * 8, 8)].astype(F32)
            at = pl.ds(pl.multiple_of(b * 64, 64), 64)
            for h in range(2):
                piece = block[:, h * 8 : h * 8 + 8, :].reshape(64, 512)
                plain[at, pl.ds(h * 512, 512)] = piece.astype(BF16)

        over(4 * half, 4 * half + 4, one)

    def scale(half):
        lanes = lax.broadcasted_iota(jnp.int32, (8, 8, 128), 2)
        sub = lax.broadcasted_iota(jnp.int32, (8, 8, 128), 1)

        def one(b):
            spread = jnp.broadcast_to(m_buf[pl.ds(b * 8, 8)], (8, 8, 128))
            mix = jnp.sum(jnp.where(lanes == sub, spread, 0.0), axis=2, keepdims=True).reshape(64, 1)
            at = pl.ds(pl.multiple_of(b * 64, 64), 64)
            for plain, mixed in ((xs, xm), (gs, gm)):
                mixed[at, :] = (plain[at, :].astype(F32) * mix).astype(BF16)

        over(4 * half, 4 * half + 4, one)

    def forward(half, group):
        rows = pl.ds(half * 256, 256)

        def one(i):
            for c in (2 * i, 2 * i + 1):
                if half == 0:
                    for n, w in enumerate((w1, w2)):
                        if group == 1:
                            src = weights(0)[n]
                            pltpu.make_async_copy(src, w.at[c], w_sem.at[2 * (c - 4) + n]).wait()
                        else:
                            pltpu.make_async_remote_copy(
                                src_ref=weights(0)[n],
                                dst_ref=w.at[c],
                                send_sem=push_send.at[2 * c + n],
                                recv_sem=push_recv.at[2 * c + n],
                                device_id=(1 - g, me),
                                device_id_type=MESH,
                            ).wait_recv()
                pre = dot(xs[rows, :], w1[c])
                cdf = 0.5 * (1.0 + lax.erf(pre * (0.5**0.5)))
                pdf = jnp.exp(-0.5 * pre * pre) * 0.3989422804014327
                hid[c, rows, :] = (pre * cdf).astype(BF16)
                dp[c, rows, :] = (cdf + pre * pdf).astype(BF16)
            acc[rows, :] += dot(hid[2 * i, rows, :], w2[2 * i]) + dot(hid[2 * i + 1, rows, :], w2[2 * i + 1])

        over(2 * group, 2 * group + 2, one)

    def backward(half, group):
        rows = pl.ds(half * 256, 256)

        def one(i):
            for c in (2 * i, 2 * i + 1):
                d_hidden = dot_t(gs[rows, :], w2[c])
                dp[c, rows, :] = (dp[c, rows, :].astype(F32) * d_hidden).astype(BF16)
            acc[rows, :] += dot_t(dp[2 * i, rows, :], w1[2 * i]) + dot_t(dp[2 * i + 1, rows, :], w1[2 * i + 1])

        over(2 * group, 2 * group + 2, one)

    def home(n, j):
        src, dst = ((pack_out, ret_out), (pack_in, ret_in))[n]
        return pltpu.make_async_remote_copy(
            src_ref=src.at[j],
            dst_ref=dst.at[me],
            send_sem=home_send.at[n, j],
            recv_sem=home_recv.at[n, j],
            device_id=(g, chip_before(me, offset_of(j))),
            device_id_type=MESH,
        )

    def own_home(n):
        src, dst = ((pack_out, ret_out), (pack_in, ret_in))[n]
        return pltpu.make_async_copy(src.at[0], dst.at[me], own_sem.at[3 + n])

    def send_home(n, half):
        target = (pack_out, pack_in)[n]

        def one(b):
            value = acc[pl.ds(pl.multiple_of(b * 64, 64), 64), :].reshape(8, 8, 1024)
            both = jnp.concatenate([value[:, :, :512], value[:, :, 512:]], axis=1)
            target[pl.ds(b * 8, 8)] = both.astype(BF16)

        over(4 * half, 4 * half + 4, one)
        if half == 0:
            own_home(n).start()
        over(1 + 31 * half, 32 + 32 * half, lambda j: home(n, j).start())

    def clear(half):
        rows = pl.ds(half * 256, 256)
        acc[rows, :] = jnp.zeros((256, 1024), F32)

    swaps = []

    def share(src, dst):
        n = len(swaps)
        swaps.append(to_sibling(src, dst, sib_send.at[n], sib_recv.at[n]))

    for half in range(2):
        rows = pl.ds(half * 256, 256)
        clear(half)
        take_in(0, half)
        unpack(0, half, xs)
        forward(half, 1)
        forward(half, 0)
        send_home(0, half)
        share(hid.at[pl.ds(0, 4), rows, :], hid_sib.at[:, rows, :])
    take_in(2, 0)
    take_in(2, 1)
    for half in range(2):
        rows = pl.ds(half * 256, 256)
        clear(half)
        take_in(1, half)
        unpack(1, half, gs)
        backward(half, 0)
        share(dp.at[pl.ds(0, 4), rows, :], dp_sib.at[:, rows, :])
        backward(half, 1)
        send_home(1, half)
        scale(half)
        share(xm.at[rows, :], xm_sib.at[rows, :])
        share(gm.at[rows, :], gm_sib.at[rows, :])

    def grad_copy(c, which):
        at = pl.ds(pl.multiple_of(c * CHUNK, CHUNK), CHUNK)
        source = stage1 if which == 0 else stage2
        target = grad_w1.at[:, at] if which == 0 else grad_w2.at[at, :]
        return pltpu.make_async_copy(source, target, grad_sem.at[which])

    for r in range(4):
        x_turn[:, pl.ds(r * 128, 128)] = xm[pl.ds(r * 128, 128), :].T
    for c in swaps:
        c.wait_recv()
    for r in range(4):
        x_turn[:, pl.ds(512 + r * 128, 128)] = xm_sib[pl.ds(r * 128, 128), :].T

    def grads(c):
        @pl.when(c > 0)
        def _():
            grad_copy(c - 1, 0).wait()

        for r in range(4):
            rows = pl.ds(r * 256, 256)
            stage1[rows, :] = (
                dot(x_turn[rows, pl.ds(0, 512)], dp[4 + c])
                + dot(x_turn[rows, pl.ds(512, 512)], dp_sib[c])
            ).astype(BF16)
        grad_copy(c, 0).start()

        @pl.when(c > 0)
        def _():
            grad_copy(c - 1, 1).wait()

        for r in range(2):
            columns = pl.ds(r * 256, 256)
            stage2[columns, :] = (
                t_dot(hid[4 + c, :, columns], gm[...]) + t_dot(hid_sib[c, :, columns], gm_sib[...])
            ).astype(BF16)
        grad_copy(c, 1).start()

    over(0, 4, grads)
    grad_copy(3, 0).wait()
    grad_copy(3, 1).wait()

    def finish(j):
        for i in range(3):
            out_copy(i, j).wait_send()
        for n in range(2):
            home(n, j).wait()

    over(1, 64, finish)
    for n in range(2):
        own_home(n).wait()
    for c in leaving:
        c.wait()
    for c in started:
        c.wait_send()


def run_layer(*args):
    sem = pltpu.SemaphoreType.DMA
    shape = jax.ShapeDtypeStruct
    return pl.pallas_call(
        layer_kernel,
        out_shape=[
            shape((64, 16, 512), BF16),
            shape((64, 16, 512), BF16),
            shape((128, 1024), BF16),
            shape((128, 3072), BF16),
            shape((128, 1024), BF16),
            shape((128, 256), F32),
            shape((1024, 2048), BF16),
            shape((2048, 1024), BF16),
        ],
        in_specs=[HBM] * 9,
        out_specs=[HBM] * 8,
        scratch_shapes=[
            pltpu.VMEM((128, 1024), BF16),
            pltpu.VMEM((128, 1024), BF16),
            pltpu.VMEM((2, 128), jnp.int32),
            pltpu.VMEM((2, 128), jnp.int32),
            pltpu.VMEM((64, 1024), BF16),
            pltpu.VMEM((128, 1024), BF16),
            pltpu.VMEM((128, 3072), BF16),
            pltpu.VMEM((128, 1024), BF16),
            pltpu.VMEM((128, 256), F32),
            pltpu.VMEM((1024, 3072), BF16),
            pltpu.VMEM((1024, 1024), BF16),
            pltpu.VMEM((128, 1024), BF16),
            pltpu.VMEM((64, 16, 512), BF16),
            pltpu.VMEM((64, 16, 512), BF16),
            pltpu.VMEM((64, 1, 128), F32),
            pltpu.VMEM((8, 1024, CHUNK), BF16),
            pltpu.VMEM((8, CHUNK, 1024), BF16),
            pltpu.VMEM((512, 1024), BF16),
            pltpu.VMEM((512, 1024), BF16),
            pltpu.VMEM((512, 1024), BF16),
            pltpu.VMEM((512, 1024), BF16),
            pltpu.VMEM((8, 512, CHUNK), BF16),
            pltpu.VMEM((8, 512, CHUNK), BF16),
            pltpu.VMEM((512, 1024), F32),
            pltpu.VMEM((64, 16, 512), BF16),
            pltpu.VMEM((64, 16, 512), BF16),
            pltpu.VMEM((512, 1024), BF16),
            pltpu.VMEM((512, 1024), BF16),
            pltpu.VMEM((4, 512, CHUNK), BF16),
            pltpu.VMEM((4, 512, CHUNK), BF16),
            pltpu.VMEM((1024, 1024), BF16),
            pltpu.VMEM((1024, CHUNK), BF16),
            pltpu.VMEM((CHUNK, 1024), BF16),
            pltpu.VMEM((64, 16, 512), BF16),
            pltpu.VMEM((64, 16, 512), BF16),
            pltpu.VMEM((64, 1, 128), F32),
            sem((12,)),
            sem((8,)),
            sem((8,)),
            sem((8,)),
            sem((3, 64)),
            sem((3, 64)),
            sem((2, 64)),
            sem((2, 64)),
            sem((5,)),
            sem((4,)),
            sem((8,)),
            sem((8,)),
            sem((2,)),
        ],
        compiler_params=pltpu.CompilerParams(
            collective_id=1, has_side_effects=True, vmem_limit_bytes=63 * 2**20
        ),
        name="layer",
    )(*args)


ORDERS = ((16, 4, 1), (4, 1, 16), (1, 16, 4))
EARLY, LATE = 384, 1024


def along(me, stride, k):
    at = (me // stride) % 4
    return me - at * stride + ((at + k) % 4) * stride


def natural_row(order, j):
    row = j % 8
    for at, stride in zip((128, 32, 8), ORDERS[order]):
        row = row + ((j // at) % 4) * (stride * 8)
    return row


def finish_kernel(*refs):
    layer_out, grad_tokens, sum_qkv, sum_proj, sum_router = refs[13:18]
    tokens, resid, att, ids_row, slots_row, ret_out, cot, mix, ret_in, w_router, w_proj, qkv, w_qkv = refs[18:31]
    rows, half_in, half_send, lhs, rhs, d_att = refs[31:37]
    parts, first, mid, second, last, third = (refs[37 + 2 * i : 39 + 2 * i] for i in range(6))
    w_sem, pair_send, pair_recv, send_sem, recv_sem = refs[49:54]
    g = lax.axis_index("group")
    me = lax.axis_index("dev")
    barrier = pltpu.get_barrier_semaphore()
    pl.semaphore_signal(barrier, inc=1, device_id=(1 - g, me), device_id_type=MESH)
    for stride in (16, 4, 1):
        for k in (1, 2, 3):
            pl.semaphore_signal(
                barrier, inc=1, device_id=(g, along(me, stride, k)), device_id_type=MESH
            )
    loads = [pltpu.make_async_copy(refs[i], refs[18 + i], w_sem.at[i]) for i in range(13)]
    for c in loads:
        c.start()

    def arrive(*which):
        for i in which:
            loads[i].wait()

    started = []

    def swap(i, src, dst):
        c = pltpu.make_async_remote_copy(
            src_ref=src,
            dst_ref=dst,
            send_sem=pair_send.at[i],
            recv_sem=pair_recv.at[i],
            device_id=(1 - g, me),
            device_id_type=MESH,
        )
        c.start()
        started.append(c)
        return c

    arrive(0, 1, 2)
    normed1, rstd1 = norm_parts(tokens[...].astype(F32))
    resid_f = resid[...].astype(F32)
    normed2, rstd2 = norm_parts(resid_f)
    half_in[0] = normed1.astype(BF16)
    half_in[1] = att[...]
    half_in[2] = normed2.astype(BF16)
    column = lax.broadcasted_iota(jnp.int32, (512, 512), 1)
    position = lax.broadcasted_iota(jnp.int32, (512, 512), 0)
    mine = pl.ds(pl.multiple_of(g * 512, 512), 512)
    theirs = pl.ds(pl.multiple_of((1 - g) * 512, 512), 512)
    for order in range(3):
        turn = (column == natural_row(order, position)).astype(F32).astype(BF16)
        for which in range(3):
            if which == 2 and order < 2:
                continue
            i = order * 2 + which
            lhs[i, :, 0:128] = dot_t(turn, half_in[which, :, mine]).astype(BF16)
            half_send[i] = dot_t(turn, half_in[which, :, theirs]).astype(BF16)
    pl.semaphore_wait(barrier, 10)
    lhs_swap = [swap(i, half_send.at[i], lhs.at[i, :, pl.ds(128, 128)]) for i in range(7)]

    def unpack(src):
        def one(i, _):
            block = src[pl.ds(i * 8, 8)].astype(F32)
            at = pl.ds(pl.multiple_of(i * 64, 64), 64)
            for h in range(2):
                piece = block[:, h * 8 : h * 8 + 8, :].reshape(64, 512)
                rows[at, pl.ds(h * 512, 512)] = piece.astype(BF16)
            return 0

        lax.fori_loop(0, 8, one, 0)

    arrive(3, 4, 5, 6, 7)
    slot = lax.broadcasted_iota(jnp.int32, (128, 128), 1)
    ids, slots = columns_of(ids_row), columns_of(slots_row)
    place = []
    for k in range(2):
        flat = ids[k] * 8 + slots[k]
        hits = [(slot + i * 128 == flat).astype(F32).astype(BF16) for i in range(4)]
        place.append(jnp.concatenate(hits, axis=1))
    place = jnp.concatenate(place, axis=0)
    grad = cot[...].astype(F32)
    mixing = [mix[:, k * 128 : k * 128 + 1] for k in range(2)]
    unpack(ret_out)
    pair = dot(place, rows[...])
    pair = [pair[:128], pair[128:]]
    layer_out[...] = (resid_f + mixing[0] * pair[0] + mixing[1] * pair[1]).astype(BF16)
    d_mix = [jnp.sum(grad * a, axis=-1, keepdims=True) for a in pair]
    centre = mixing[0] * d_mix[0] + mixing[1] * d_mix[1]
    expert = lax.broadcasted_iota(jnp.int32, (128, 128), 1)
    d_logits = sum(
        jnp.where(expert == ids[k], mixing[k] * (d_mix[k] - centre), 0.0) for k in range(2)
    ).astype(BF16)
    arrive(8, 9)
    unpack(ret_in)
    pair = dot(place, rows[...])
    d_normed2 = (
        mixing[0] * pair[:128] + mixing[1] * pair[128:] + dot(d_logits[:, :64], w_router[...])
    )
    d_resid = grad + norm_backward(normed2, rstd2, d_normed2)
    own_rows, sib_rows = pl.ds(0, 128), pl.ds(128, 128)
    rhs[own_rows, pl.ds(3072, 1024)] = d_resid.astype(BF16)
    rhs[own_rows, pl.ds(4096, 128)] = d_logits
    tail = pl.ds(3072, 1152)
    early_swap = swap(7, rhs.at[own_rows, tail], rhs.at[sib_rows, tail])
    arrive(10)
    d_att[...] = dot_t(rhs[own_rows, pl.ds(3072, 1024)], w_proj[...]).astype(BF16)

    def place_of(phase, order):
        return (me // ORDERS[order][phase]) % 4

    def launch(phase, late, order, src, dst):
        stride = ORDERS[order][phase]
        at = place_of(phase, order)
        group = []
        for k in (1, 2, 3):
            sem = ((phase * 2 + late) * 3 + order) * 3 + k - 1
            c = pltpu.make_async_remote_copy(
                src_ref=src.at[order, (at + k) % 4],
                dst_ref=dst.at[order, k - 1],
                send_sem=send_sem.at[sem],
                recv_sem=recv_sem.at[sem],
                device_id=(g, along(me, stride, k)),
                device_id_type=MESH,
            )
            c.start()
            group.append(c)
        started.extend(group)
        return group

    def sum_one(late, order, arriving):
        for c in arriving:
            c.wait_recv()
        at = place_of(0, order)
        for q in range(4):
            piece = pl.ds(q * 32, 32)
            total = parts[late][order, at, piece, :].astype(F32)
            for k in range(3):
                total = total + first[late][order, k, piece, :].astype(F32)
            mid[late][order, q] = total.astype(BF16)
        return launch(1, late, order, mid[late], second[late])

    def sum_two(late, order, arriving):
        for c in arriving:
            c.wait_recv()
        total = mid[late][order, place_of(1, order)].astype(F32)
        for k in range(3):
            total = total + second[late][order, k].astype(F32)
        for q in range(4):
            last[late][order, q] = total[q * 8 : q * 8 + 8, :]
        return launch(2, late, order, last[late], third[late])

    def sum_three(late, order, arriving):
        for c in arriving:
            c.wait_recv()
        total = last[late][order, place_of(2, order)]
        for k in range(3):
            total = total + third[late][order, k]
        return total

    for c in lhs_swap:
        c.wait_recv()
    early_swap.wait_recv()
    early = []
    for order in range(3):
        for r in range(4):
            for left, at, width in (
                (order * 2 + 1, 0, EARLY if order < 2 else 256),
                (6, 256, 128),
            ):
                if left == 6 and order < 2:
                    continue
                value = dot(
                    lhs[left, r * 128 : r * 128 + 128, :],
                    rhs[:, 3072 + order * EARLY + at : 3072 + order * EARLY + at + width],
                )
                parts[0][order, r, :, pl.ds(at, width)] = value.astype(BF16)
        early.append(launch(0, 0, order, parts[0], first[0]))

    arrive(11)
    masks = head_masks()
    for p in range(8):
        q2, k2, v2 = (qkv[:, i * 1024 + p * 128 : i * 1024 + p * 128 + 128] for i in range(3))
        d2 = d_att[:, p * 128 : p * 128 + 128]
        k_two, v_two = two_heads(k2, masks), two_heads(v2, masks)
        probs = softmax_pair(dot_t(q2, k_two) * 0.125)
        d_probs = dot_t(d2, v_two)
        d_scores = []
        for h in range(2):
            one = d_probs[:, h * 128 : h * 128 + 128]
            one = probs[h] * (one - jnp.sum(probs[h] * one, axis=-1, keepdims=True))
            d_scores.append(one * 0.125)
        d_scores = jnp.concatenate(d_scores, axis=1).astype(BF16)
        probs = jnp.concatenate(probs, axis=1).astype(BF16)
        d_k = t_dot(d_scores, q2)
        d_v = t_dot(probs, d2)
        rhs[own_rows, pl.ds(p * 128, 128)] = dot(d_scores, k_two).astype(BF16)
        rhs[own_rows, pl.ds(1024 + p * 128, 128)] = (
            d_k[:128] * masks[0] + d_k[128:] * masks[1]
        ).astype(BF16)
        rhs[own_rows, pl.ds(2048 + p * 128, 128)] = (
            d_v[:128] * masks[0] + d_v[128:] * masks[1]
        ).astype(BF16)
    late_swap = []
    for order in range(3):
        at = pl.ds(order * LATE, LATE)
        late_swap.append(swap(8 + order, rhs.at[own_rows, at], rhs.at[sib_rows, at]))
    early = [sum_one(0, order, early[order]) for order in range(3)]
    late = []
    for order in range(3):
        late_swap[order].wait_recv()
        for r in range(4):
            value = dot(
                lhs[order * 2, r * 128 : r * 128 + 128, :], rhs[:, order * LATE : order * LATE + LATE]
            )
            parts[1][order, r] = value.astype(BF16)
        late.append(launch(0, 1, order, parts[1], first[1]))
    early = [sum_two(0, order, early[order]) for order in range(3)]
    arrive(12)
    d_normed1 = dot_t(rhs[own_rows, pl.ds(0, 3072)], w_qkv[...])
    grad_tokens[...] = (d_resid + norm_backward(normed1, rstd1, d_normed1)).astype(BF16)
    late = [sum_one(1, order, late[order]) for order in range(3)]
    sum_proj[:, 0:384] = sum_three(0, 0, early[0])
    sum_proj[:, 384:768] = sum_three(0, 1, early[1])
    tail_sum = sum_three(0, 2, early[2])
    sum_proj[:, 768:1024] = tail_sum[:, :256]
    sum_router[...] = tail_sum[:, 256:320]
    late = [sum_two(1, order, late[order]) for order in range(3)]
    for order in range(3):
        sum_qkv[:, order * LATE : order * LATE + LATE] = sum_three(1, order, late[order])
    for c in started:
        c.wait_send()


def run_finish(*args):
    sem = pltpu.SemaphoreType.DMA
    shape = jax.ShapeDtypeStruct
    scratch = [pltpu.VMEM(a.shape, a.dtype) for a in args]
    scratch += [
        pltpu.VMEM((512, 1024), BF16),
        pltpu.VMEM((3, 128, 1024), BF16),
        pltpu.VMEM((7, 512, 128), BF16),
        pltpu.VMEM((7, 512, 256), BF16),
        pltpu.VMEM((256, 4224), BF16),
        pltpu.VMEM((128, 1024), BF16),
    ]
    for lead, kind in (
        ((3, 4, 128), BF16),
        ((3, 3, 128), BF16),
        ((3, 4, 32), BF16),
        ((3, 3, 32), BF16),
        ((3, 4, 8), F32),
        ((3, 3, 8), F32),
    ):
        scratch += [pltpu.VMEM(lead + (width,), kind) for width in (EARLY, LATE)]
    scratch += [sem((13,)), sem((11,)), sem((11,)), sem((54,)), sem((54,))]
    return pl.pallas_call(
        finish_kernel,
        out_shape=[
            shape((128, 1024), BF16),
            shape((128, 1024), BF16),
            shape((8, 3072), F32),
            shape((8, 1024), F32),
            shape((8, 64), F32),
        ],
        in_specs=[HBM] * 13,
        out_specs=[VMEM] * 5,
        scratch_shapes=scratch,
        compiler_params=pltpu.CompilerParams(
            collective_id=3, has_side_effects=True, vmem_limit_bytes=53 * 2**20
        ),
        name="finish",
    )(*args)


def store_kernel(*refs):
    srcs, dsts, sems = refs[:7], refs[7:14], refs[14]
    copies = [pltpu.make_async_copy(srcs[i], dsts[i], sems.at[i]) for i in range(5)]
    for i in (5, 6):
        rows = srcs[i].shape[0] // 8
        for j in range(8):
            at = pl.ds(j * rows, rows)
            sem = sems.at[5 + (i - 5) * 8 + j]
            copies.append(pltpu.make_async_copy(srcs[i].at[at, :], dsts[i].at[at, :], sem))
    for c in copies:
        c.start()
    for c in copies:
        c.wait()


def run_store(*arrays):
    return pl.pallas_call(
        store_kernel,
        out_shape=[jax.ShapeDtypeStruct(a.shape, a.dtype) for a in arrays],
        in_specs=[VMEM] * 5 + [VMEM] * 2,
        out_specs=[HBM] * 7,
        scratch_shapes=[pltpu.SemaphoreType.DMA((21,))],
        compiler_params=pltpu.CompilerParams(vmem_limit_bytes=12 * 2**20),
        name="store",
    )(*arrays)


def shards(tokens, cotangent, expert_ids, slot_ids, w_qkv, w_proj, w_router, w_in, w_out):
    ids, slots, router = expert_ids.T, slot_ids.T, w_router.T
    returned_out, returned_in, resid, qkv, att, mix, grad_w_in, grad_w_out = run_layer(
        tokens, cotangent, ids, slots, w_qkv, w_proj, router, w_in[0], w_out[0]
    )
    small = run_finish(
        tokens, resid, att, ids, slots, returned_out, cotangent, mix, returned_in, router, w_proj, qkv, w_qkv
    )
    layer_out, grad_tokens, sum_qkv, sum_proj, sum_router, grad_w_in, grad_w_out = run_store(
        *small, grad_w_in, grad_w_out
    )
    return (
        layer_out,
        grad_tokens,
        sum_qkv,
        sum_proj,
        sum_router,
        grad_w_in[None],
        grad_w_out[None],
    )


def solution(mesh):
    return jax.shard_map(
        shards,
        mesh=mesh,
        in_specs=(
            P(("group", "dev"), None),
            P(("group", "dev"), None),
            P(("group", "dev"), None),
            P(("group", "dev"), None),
            P(),
            P(),
            P(),
            P("dev", None, "group"),
            P("dev", "group", None),
        ),
        out_specs=(
            P(("group", "dev"), None),
            P(("group", "dev"), None),
            P(("group", "dev"), None),
            P(("group", "dev"), None),
            P(("group", "dev"), None),
            P("dev", None, "group"),
            P("dev", "group", None),
        ),
        check_vma=False,
    )
```

time: 162 us -> 131 us (0.81)
  local copies, waits for them, and re-layouts: 23.7 us -> 0.92 us
  Pallas kernels: 136 us -> 128 us
    unnamed x38 -> x12, local copies, waits for them, and re-layouts: 23.6 us -> 0.92 us
    pallas_call x2, Pallas kernels: 95.4 us -> 84.5 us  [the longest x1 80.8 us: run_layer(): pl.pallas_call(layer_kernel, out_shape=[shape((64, 16, 512), BF16), shape...]
    pallas_call x1, Pallas kernels: 40.3 us -> 43.9 us  [run_finish(): pl.pallas_call(finish_kernel, out_shape=[shape((128, 1024), BF16), shape(...]
  transfers between devices with their start and end apart: 2 -> 0, of which waited for: 0 -> 0; matrix products, arithmetic and copies ran while one was open for 2% -> 0% of each run, Pallas kernels for 26% -> 0%
where the time goes in v2:
time: 131 us; the launch traced here: 130 us
  Pallas kernels  128 us (98%)
    pallas_call x1, Pallas kernels, run_layer(): pl.pallas_call(layer_kernel, out_shape=[shape((64, 16, 512), BF16), shape...  80.8 us
    pallas_call x1, Pallas kernels, run_finish(): pl.pallas_call(finish_kernel, out_shape=[shape((128, 1024), BF16), shape(...  43.9 us
    pallas_call x1, Pallas kernels, run_store(): pl.pallas_call(store_kernel, out_shape=[jax.ShapeDtypeStruct(a.shape, a.d...  3.67 us

profile of v2, /device:TPU:0, one launch (start us, length us, event | category | flops | bytes accessed | tf_op | source)
XLA Modules:
  0.0 130.3 jit_solution(16937435442117338890)
XLA Ops:
  0.6 0.0 copy-start.2
  0.6 0.0 copy-start.4
  0.7 0.0 copy-start.5
  0.7 80.8 %layer.1 = (bf16[64,16,512]{2,1,0:T(8,128)(2,1)}, bf16[64,16,512]{2,1,0:T(8,128)(2,1)}, bf16[128,1024]{1,0:T(8,128)(2,1)}, bf16[128,3072]{1,0:T(8,128)(2,1)}, bf...) custom-call(bf16[128,1024]{1,0:T(8,128)(2,1)} %refs_0_.3, ...), custom_call_target="tpu_custom_call" | custom-call | tf_op jit(solution)/shard_map/layer/pallas_call | solution.py:443
  81.5 0.0 copy-done.2
  81.5 0.0 copy-done.4
  81.5 0.0 copy-done.5
  81.5 0.0 copy-start.3
  81.6 0.9 copy-done.3
  82.5 0.0 copy-start
  82.5 0.0 copy-start.1
  82.5 43.9 %finish.1 = (bf16[128,1024]{1,0:T(8,128)(2,1)S(1)}, bf16[128,1024]{1,0:T(8,128)(2,1)S(1)}, f32[8,3072]{1,0:T(8,128)S(1)}, f32[8,1024]{1,0:T(8,128)S(1)}, f32[8,64]{1,0:T(8,128)S(1)}) custom-call(bf16[128,1024]{1,0:T(8,128)(2,1)} %refs_0_.3, bf16[128,1024]{1,0:T(8,128)(2,1)} %get-tuple-element.27.refs_1_, bf16[128,1024]{1,0:T(8,128)(2,1)} %get-tuple-element.28.refs_2_, ...), custom_call_target="tpu_custom_call" | custom-call | tf_op jit(solution)/shard_map/finish/pallas_call | solution.py:786
  126.4 0.0 copy-done
  126.4 0.0 copy-done.1
  126.4 3.7 %store.1 = (bf16[128,1024]{1,0:T(8,128)(2,1)}, bf16[128,1024]{1,0:T(8,128)(2,1)}, f32[8,3072]{1,0:T(8,128)}, f32[8,1024]{1,0:T(8,128)}, f32[8,64]{1,0:T(8,128)},...) custom-call(bf16[128,1024]{1,0:T(8,128)(2,1)S(1)} %get-tuple-element.33.refs_0_, ...), custom_call_target="tpu_custom_call" | custom-call | tf_op jit(solution)/shard_map/store/pallas_call | solution.py:821
Async XLA Ops:
  0.6 80.9 %copy-start.2 = (bf16[1024,64]{0,1:T(8,128)(2,1)S(1)}, bf16[1024,64]{0,1:T(8,128)(2,1)}, u32[]{:S(2)}) copy-start(bf16[1024,64]{0,1:T(8,128)(2,1)} %param.15) | copy-start | bytes 393220
  0.6 80.9 %copy-start.4 = (s32[128,2]{0,1:T(2,128)S(1)}, s32[128,2]{0,1:T(2,128)}, u32[]{:S(2)}) copy-start(s32[128,2]{0,1:T(2,128)} %param.11) | copy-start | bytes 3076
  0.7 80.9 %copy-start.5 = (s32[128,2]{0,1:T(2,128)S(1)}, s32[128,2]{0,1:T(2,128)}, u32[]{:S(2)}) copy-start(s32[128,2]{0,1:T(2,128)} %param.12) | copy-start | bytes 3076
  81.5 0.9 copy-start.3
  82.5 44.0 %copy-start = (bf16[1024,2048]{1,0:T(8,128)(2,1)S(1)}, bf16[1024,2048]{1,0:T(8,128)(2,1)}, u32[]{:S(2)}) copy-start(bf16[1024,2048]{1,0:T(8,128)(2,1)} %get-tuple-element.38.refs_5_) | copy-start | bytes 12582916
  82.5 44.0 %copy-start.1 = (bf16[2048,1024]{1,0:T(8,128)(2,1)S(1)}, bf16[2048,1024]{1,0:T(8,128)(2,1)}, u32[]{:S(2)}) copy-start(bf16[2048,1024]{1,0:T(8,128)(2,1)} %get-tuple-element.39.refs_6_) | copy-start | bytes 12582916
